TPU v7x, 128 devices: a whole 4x4x4 slice. The times are simulated.
128 devices in a mesh: row: 16 (over x_hi, z, core), col: 8 (over x_lo, y).
Axes of the slice: x: 4 (x_hi: 2, x_lo: 2; x = x_hi * 2 + x_lo), y: 4, z: 4, core: 2. Of those that a mesh axis runs over, the one named last changes fastest.
Arguments:
- features: bfloat16 [512, 512, 180], P('row', 'col'), may hold values from -6 to 6
- cotangent: bfloat16 [512, 512, 180], P('row', 'col'), may hold values from -6 to 6
- w_qkv: bfloat16 [180, 540], replicated, may hold values from -8 to 8
- w_proj: bfloat16 [180, 180], replicated, may hold values from -0.4375 to 0.4375
- w_fc1: bfloat16 [180, 360], replicated, may hold values from -0.4375 to 0.4375
- w_fc2: bfloat16 [360, 180], replicated, may hold values from -0.3125 to 0.3125
- w_conv: bfloat16 [9, 180, 180], replicated, may hold values from -0.15625 to 0.15625
- gain_attn: float32 [180], replicated, may hold values from 0.25 to 1.75
- gain_mlp: float32 [180], replicated, may hold values from 0.25 to 1.75
- pos_table: float32 [225, 6], replicated, may hold values from -4 to 4
Outputs:
- d_features: bfloat16 [512, 512, 180], P('row', 'col')
- grad_qkv: float32 [180, 540], replicated
- grad_proj: float32 [180, 180], replicated
- grad_fc1: float32 [180, 360], replicated
- grad_fc2: float32 [360, 180], replicated
- grad_conv: float32 [9, 180, 180], replicated
All inputs are finite; a program needn't handle non-finite values.
Results may differ from a plain program's by a relative error of at most 0.025.
The roundings to bfloat16 on the way count: a program that leaves them out, or rounds other values in their place, can miss the bound.
Values may be sent and summed in bfloat16 or wider, within the bound.
A program may use at most 128 MiB of HBM per device.

v0:
```python
import math

import jax
import jax.numpy as jnp
from jax import lax
from jax.experimental import pallas as pl
from jax.experimental.pallas import tpu as pltpu
from jax.sharding import PartitionSpec as P

C = 180
CP = 192
HEADS = 6
HD = 30
HP = 32
FF = 360
WIN = 8
SHIFT = 4
ROWS = 32
COLS = 64
BLK = 16
NBLK = COLS // BLK
TOK = ROWS * BLK
PAIR = WIN * BLK
FULL = 19
HALF = 7
GROWS = (FULL + HALF) * CP
BF = jnp.bfloat16
F32 = jnp.float32
MESH = pl.DeviceIdType.MESH
VMEM = pltpu.VMEM


def iota(shape, dim):
    return lax.broadcasted_iota(jnp.int32, shape, dim)


def nn(a, b):
    return lax.dot_general(a, b, (((1,), (0,)), ((), ())), preferred_element_type=F32)


def nt(a, b):
    return lax.dot_general(a, b, (((1,), (1,)), ((), ())), preferred_element_type=F32)


def low(a):
    return a.astype(BF)


def eye(rows, cols):
    return low(jnp.where(iota((rows, cols), 0) == iota((rows, cols), 1), 1.0, 0.0))


def spread(padded, plain, pad_dim):
    shape = (padded, plain) if pad_dim == 0 else (plain, padded)
    p = iota(shape, pad_dim)
    c = iota(shape, 1 - pad_dim)
    hit = ((p & (HP - 1)) < HD) & (c == (p >> 5) * HD + (p & (HP - 1)))
    return low(jnp.where(hit, 1.0, 0.0))


def exchange_in(f_ref, g_ref, fr_ref, gr_ref, strip_ref, corner_ref, mine, send, recv):
    row, col = lax.axis_index("row"), lax.axis_index("col")
    n_row, n_col = lax.axis_size("row"), lax.axis_size("col")
    up, down = lax.rem(row + n_row - 1, n_row), lax.rem(row + 1, n_row)
    left, right = lax.rem(col + n_col - 1, n_col), lax.rem(col + 1, n_col)
    barrier = pltpu.get_barrier_semaphore()
    for peer in ((down, col), (row, right), (down, right)):
        pl.semaphore_signal(barrier, inc=1, device_id=peer, device_id_type=MESH)
    fs = f_ref[:, 0:16, :].astype(F32)[:, 0:8, :]
    gs = g_ref[:, 0:16, :].astype(F32)[:, 0:8, :]
    both = jnp.where(iota((ROWS, 8, C), 1) < 4, fs, pltpu.roll(gs, 4, 1))
    mine[32:288, :] = low(both.reshape(ROWS * 8, C))
    mine[0:32, :] = low(gs[:, 4, :])
    pl.semaphore_wait(barrier, 3)
    pairs = (
        (f_ref.at[0:4], fr_ref, (up, col)),
        (g_ref.at[0:5], gr_ref, (up, col)),
        (mine, strip_ref, (row, left)),
        (mine.at[0:80], corner_ref, (up, left)),
    )
    copies = []
    for i, (src, dst, peer) in enumerate(pairs):
        copies.append(
            pltpu.make_async_remote_copy(
                src_ref=src,
                dst_ref=dst,
                send_sem=send.at[i],
                recv_sem=recv.at[i],
                device_id=peer,
                device_id_type=MESH,
            )
        )
        copies[-1].start()
    for copy in copies:
        copy.wait()


def call_exchange_in(features, cotangent):
    return pl.pallas_call(
        exchange_in,
        out_shape=(
            jax.ShapeDtypeStruct((4, COLS, C), BF),
            jax.ShapeDtypeStruct((5, COLS, C), BF),
            jax.ShapeDtypeStruct((288, C), BF),
            jax.ShapeDtypeStruct((80, C), BF),
        ),
        in_specs=[pl.BlockSpec(memory_space=VMEM)] * 2,
        out_specs=[pl.BlockSpec(memory_space=VMEM)] * 4,
        scratch_shapes=[
            VMEM((288, C), BF),
            pltpu.SemaphoreType.DMA((4,)),
            pltpu.SemaphoreType.DMA((4,)),
        ],
        compiler_params=pltpu.CompilerParams(
            collective_id=0, has_side_effects=True, vmem_limit_bytes=32 * 2**20
        ),
        name="exchange_in",
    )(features, cotangent)


def column(gain_ref):
    wide = jnp.where(iota((CP, C), 0) == iota((CP, C), 1), gain_ref[...], 0.0)
    return jnp.sum(wide, axis=1, keepdims=True)


def moments(values):
    mean = jnp.sum(values[:C], axis=0, keepdims=True) * (1.0 / C)
    centred = values - mean
    inner = centred[:C]
    var = jnp.sum(inner * inner, axis=0, keepdims=True) * (1.0 / C)
    return centred, lax.rsqrt(var + 1e-05)


def norm_back(upstream, normed, inverse, gain):
    scaled = upstream * gain
    first = jnp.sum(scaled, axis=0, keepdims=True) * (1.0 / C)
    second = jnp.sum(scaled * normed, axis=0, keepdims=True) * (1.0 / C)
    return inverse * (scaled - first - normed * second)


def gelu_parts(x):
    u = jnp.abs(x) * math.sqrt(0.5)
    t = 1.0 / (1.0 + 0.3275911 * u)
    e = jnp.exp(-u * u)
    poly = t * (
        0.254829592
        + t * (-0.284496736 + t * (1.421413741 + t * (-1.453152027 + t * 1.061405429)))
    )
    tail = 0.5 * poly * e
    cdf = jnp.where(x >= 0.0, 1.0 - tail, tail)
    return cdf, e * (1.0 / math.sqrt(2.0 * math.pi))


def fold(scores, second):
    parts = scores.reshape(WIN, 2, WIN, PAIR)
    return jnp.where(second, parts[:, 1], parts[:, 0]).reshape(WIN * WIN, PAIR)


def unfold(probs, second):
    parts = probs.reshape(WIN, WIN, PAIR)
    zero = jnp.zeros_like(parts)
    both = jnp.stack([jnp.where(second, zero, parts), jnp.where(second, parts, zero)], axis=1)
    return low(both.reshape(PAIR, PAIR))


def two_heads(block):
    zero = jnp.zeros((HP, PAIR), BF)
    top = jnp.concatenate([block[:HP], zero], axis=1)
    return jnp.concatenate([top, jnp.concatenate([zero, block[HP:]], axis=1)], axis=0)


def own_heads(product):
    return jnp.concatenate([product[:HP, :PAIR], product[HP:, PAIR:]], axis=0)


def compute(
    f_ref, g_ref, fr_ref, gr_ref, strip_ref, corner_ref,
    wqkv_ref, wproj_ref, w1_ref, w2_ref, wconv_ref, g1_ref, g2_ref, d_ref,
    out_ref, grads_ref,
    xs, gs, wqkvt, wqkvp, wprojt, wprojp, w1t, w1p, w2t, w2p, wcp, bias,
    packed, attended, probs, knat, vnat, dheads, dpacked,
    a_conv, a_proj, a_fc1, a_fc2, a_qkv,
):
    row, col = lax.axis_index("row"), lax.axis_index("col")
    last_row = row == lax.axis_size("row") - 1
    last_col = col == lax.axis_size("col") - 1
    factor = HD**-0.5

    pad = eye(CP, C)
    sel, sel_one = spread(3 * CP, 3 * C, 0), spread(CP, C, 0)
    wq = low(nn(pad, wqkv_ref[...]))
    wqkvt[...] = low(nt(sel, wq))
    wqkvp[...] = low(nt(wq, sel))
    turned = low(nt(pad, wproj_ref[...]))
    wprojt[...] = low(nt(turned, sel_one))
    wprojp[...] = low(nt(sel_one, turned))
    w1p[...] = low(nn(pad, w1_ref[...]))
    w1t[...] = low(nt(eye(FF, FF), w1p[...]))
    w2t[...] = low(nt(pad, w2_ref[...]))
    w2p[...] = low(nn(w2_ref[...], eye(C, CP)))
    for t in range(9):
        wcp[t] = low(nn(pad, wconv_ref[t]))
    gain1, gain2 = column(g1_ref), column(g2_ref)
    for h in range(HEADS):
        table = d_ref[h]
        for kr in range(WIN):
            start = (WIN - 1 - kr) * BLK
            bias[h, kr * WIN : (kr + 1) * WIN, :] = table[:, start : start + PAIR]
    for acc in (a_conv, a_proj, a_fc1, a_fc2, a_qkv):
        acc[...] = jnp.zeros_like(acc)

    sub = iota((8, C), 0)

    def tail(body, last):
        return jnp.concatenate([body[:56], last], axis=0)

    def put_x(i, v, extra):
        rolled = pltpu.roll(v, 60, 0)
        full = low(tail(rolled, jnp.where(sub < 4, rolled[56:], pltpu.roll(extra, 4, 0))))
        for b in range(NBLK):
            xs[b, pl.ds(pl.multiple_of(i * BLK, BLK), BLK), :] = full[b * BLK : (b + 1) * BLK]

    keep0 = jnp.where((sub == 3) & last_col, 0.0, 1.0)
    keep2 = jnp.where((sub == 4) & last_col, 0.0, 1.0)

    def put_g(i, v, extra, fifth):
        r5, r4, r3 = pltpu.roll(v, 59, 0), pltpu.roll(v, 60, 0), pltpu.roll(v, 61, 0)
        e5 = jnp.where(sub == 7, fifth, pltpu.roll(extra, 7, 0))
        l5 = jnp.where(sub < 3, r5[56:], e5) * keep0
        l4 = jnp.where(sub < 4, r4[56:], extra)
        l3 = jnp.where(sub < 5, r3[56:], pltpu.roll(extra, 1, 0)) * keep2
        for k, (r, last) in enumerate(((r5, l5), (r4, l4), (r3, l3))):
            full = low(tail(r, last))
            for b in range(NBLK):
                gs[k, b, pl.ds(pl.multiple_of(i * BLK, BLK), BLK), :] = full[
                    b * BLK : (b + 1) * BLK
                ]

    extras = strip_ref[32:288, :].astype(F32).reshape(ROWS, 8, C)
    fifths = strip_ref[0:32, :].astype(F32)
    c_extras = corner_ref[32:80, :].astype(F32).reshape(6, 8, C)
    c_fifths = corner_ref[0:16, :].astype(F32)
    for i in range(ROWS):
        if i < ROWS - 4:
            put_x(i, f_ref[i + 4].astype(F32), extras[i + 4])
        else:
            put_x(i, fr_ref[i - 28].astype(F32), c_extras[i - 28])
    for i in range(ROWS + 2):
        if i < ROWS - 3:
            put_g(i, g_ref[i + 3].astype(F32), extras[i + 3], fifths[i + 3 : i + 4])
        else:
            k = i - 29
            put_g(i, gr_ref[k].astype(F32), c_extras[k], c_fifths[k : k + 1])

    lane = iota((1, PAIR), 1)
    second = ((lane >> 3) & 1) == 1
    ones_pair = eye(PAIR, PAIR)
    k_sub, q_lane = iota((WIN * WIN, PAIR), 0), iota((WIN * WIN, PAIR), 1)
    rows_differ = ((k_sub >> 5) & 1) != ((q_lane >> 6) & 1)
    cols_differ = (((k_sub >> 2) & 1) != ((q_lane >> 2) & 1)) & (((q_lane >> 3) & 1) == 1)
    tok = iota((1, TOK), 1) >> 4
    drop0 = (tok == 27) & last_row
    drop2 = (tok == 28) & last_row

    def block(b, carry):
        x = nt(eye(CP, C), xs[b])
        centred, inv1 = moments(x)
        normed1 = centred * inv1
        n1 = low(normed1 * gain1)
        packed[...] = low(nn(wqkvt[...], n1))
        col_flag = last_col & (b == NBLK - 1)

        def attend(a, carry):
            lanes = pl.ds(pl.multiple_of(a * PAIR, PAIR), PAIR)
            row_flag = last_row & (a == ROWS // WIN - 1)
            mask = jnp.where((rows_differ & row_flag) | (cols_differ & col_flag), -100.0, 0.0)
            for j in range(HEADS // 2):
                q = packed[64 * j : 64 * j + 64, lanes]
                k = packed[CP + 64 * j : CP + 64 * j + 64, lanes]
                v = packed[2 * CP + 64 * j : 2 * CP + 64 * j + 64, lanes]
                kn = low(nt(ones_pair, k))
                knat[a, j] = kn
                vnat[a, j] = low(nt(ones_pair, v))
                scores = nn(kn, two_heads(q))
                wide = []
                for s in range(2):
                    sc = fold(scores[:, s * PAIR : (s + 1) * PAIR], second)
                    sc = sc * factor + bias[2 * j + s] + mask
                    e = jnp.exp(sc - jnp.max(sc, axis=0, keepdims=True))
                    p = e * (1.0 / jnp.sum(e, axis=0, keepdims=True))
                    probs[a, 2 * j + s] = p
                    wide.append(unfold(p, second))
                o = nn(v, jnp.concatenate(wide, axis=1))
                attended[64 * j : 64 * j + 64, lanes] = low(own_heads(o))
            return carry

        lax.fori_loop(0, ROWS // WIN, attend, 0)

        middle = x + nn(wprojt[...], attended[...])
        centred2, inv2 = moments(middle)
        normed2 = centred2 * inv2
        n2 = low(normed2 * gain2)
        pre = nn(w1t[...], n2)
        cdf, pdf = gelu_parts(pre)
        hidden = low(pre * cdf)
        slope = cdf + pre * pdf
        z = low(middle + nn(w2t[...], hidden))

        z0 = jnp.where(drop0, 0.0, z.astype(F32)).astype(BF)
        z2 = jnp.where(drop2, 0.0, z.astype(F32)).astype(BF)
        total = jnp.zeros((CP, TOK), F32)
        for dy in range(3):
            part = jnp.zeros((CP, TOK), F32)
            zd = (z0, z, z2)[dy]
            for dx in range(3):
                source = gs[dx, b, (2 - dy) * BLK : (2 - dy) * BLK + TOK, :]
                part = part + nt(wcp[3 * dy + dx], source)
                a_conv[3 * dy + dx] += nn(zd, source)
            if dy == 0:
                part = jnp.where(drop0, 0.0, part)
            if dy == 2:
                part = jnp.where(drop2, 0.0, part)
            total = total + part
        d_shift = low(total)

        a_fc2[:FF, :] += nt(hidden, d_shift)
        d_pre = low(nn(w2p[...], d_shift) * slope)
        a_fc1[:, :FF] += nt(n2, d_pre)
        d_middle = d_shift.astype(F32) + norm_back(nn(w1p[...], d_pre), normed2, inv2, gain2)
        d_attn = low(d_middle)
        a_proj[...] += nt(attended[...], d_attn)
        dheads[...] = low(nn(wprojp[...], d_attn))

        def attend_back(a, carry):
            lanes = pl.ds(pl.multiple_of(a * PAIR, PAIR), PAIR)
            for j in range(HEADS // 2):
                q = packed[64 * j : 64 * j + 64, lanes]
                k = packed[CP + 64 * j : CP + 64 * j + 64, lanes]
                do = dheads[64 * j : 64 * j + 64, lanes]
                d_prob = nn(vnat[a, j], two_heads(do))
                p_wide, s_wide = [], []
                for s in range(2):
                    p = probs[a, 2 * j + s]
                    dp = fold(d_prob[:, s * PAIR : (s + 1) * PAIR], second)
                    ds = p * (dp - jnp.sum(p * dp, axis=0, keepdims=True)) * factor
                    p_wide.append(unfold(p, second))
                    s_wide.append(unfold(ds, second))
                dv = nt(do, jnp.concatenate(p_wide, axis=0))
                dq = nn(k, jnp.concatenate(s_wide, axis=1))
                dk = nt(q, jnp.concatenate(s_wide, axis=0))
                dpacked[64 * j : 64 * j + 64, lanes] = low(own_heads(dq))
                dpacked[CP + 64 * j : CP + 64 * j + 64, lanes] = low(own_heads(dk))
                dpacked[2 * CP + 64 * j : 2 * CP + 64 * j + 64, lanes] = low(own_heads(dv))
            return carry

        lax.fori_loop(0, ROWS // WIN, attend_back, 0)

        a_qkv[...] += nt(n1, dpacked[...])
        d_in = d_middle + norm_back(nn(wqkvp[...], dpacked[...]), normed1, inv1, gain1)
        d_low = low(d_in)
        for a in range(ROWS // WIN):
            natural = nt(ones_pair, d_low[:, a * PAIR : (a + 1) * PAIR])
            out_ref[b, a * PAIR : (a + 1) * PAIR, :] = low(natural[:, :C])
        return carry

    lax.fori_loop(0, NBLK, block, 0)

    rests = []
    place = 0

    def put(tile):
        nonlocal place
        grads_ref[place * CP : (place + 1) * CP, :] = low(tile)
        place += 1

    half_zero = jnp.zeros((CP, 64), F32)
    for t in range(9):
        put(a_conv[t, :, 0:128])
        rests.append(jnp.concatenate([a_conv[t, :, 128:C], half_zero[:, : 64 - (C - 128)]], axis=1))
    put(a_proj[:, 0:128])
    rests.append(a_proj[:, 128:192])
    for i in range(2):
        put(a_fc2[i * CP : (i + 1) * CP, 0:128])
        rests.append(a_fc2[i * CP : (i + 1) * CP, 128:192])
    for i in range(3):
        put(a_fc1[:, i * 128 : (i + 1) * 128])
    for i in range(4):
        put(a_qkv[:, i * 128 : (i + 1) * 128])
    rests.append(a_qkv[:, 512:576])
    rests.append(half_zero)
    for i in range(HALF):
        put(jnp.concatenate([rests[2 * i], rests[2 * i + 1]], axis=1))


def call_compute(features, cotangent, halo, w_qkv, w_proj, w_fc1, w_fc2, w_conv, g1, g2, table):
    scratch = [
        VMEM((NBLK, TOK, C), BF),
        VMEM((3, NBLK, (ROWS + 2) * BLK, C), BF),
        VMEM((3 * CP, CP), BF),
        VMEM((CP, 3 * CP), BF),
        VMEM((CP, CP), BF),
        VMEM((CP, CP), BF),
        VMEM((FF, CP), BF),
        VMEM((CP, FF), BF),
        VMEM((CP, FF), BF),
        VMEM((FF, CP), BF),
        VMEM((9, CP, C), BF),
        VMEM((HEADS, WIN * WIN, PAIR), F32),
        VMEM((3 * CP, TOK), BF),
        VMEM((CP, TOK), BF),
        VMEM((ROWS // WIN, HEADS, WIN * WIN, PAIR), F32),
        VMEM((ROWS // WIN, HEADS // 2, PAIR, 64), BF),
        VMEM((ROWS // WIN, HEADS // 2, PAIR, 64), BF),
        VMEM((CP, TOK), BF),
        VMEM((3 * CP, TOK), BF),
        VMEM((9, CP, C), F32),
        VMEM((CP, CP), F32),
        VMEM((CP, 384), F32),
        VMEM((384, CP), F32),
        VMEM((CP, 3 * CP), F32),
    ]
    return pl.pallas_call(
        compute,
        out_shape=(
            jax.ShapeDtypeStruct((NBLK, TOK, C), BF),
            jax.ShapeDtypeStruct((GROWS, 128), BF),
        ),
        in_specs=[pl.BlockSpec(memory_space=VMEM)] * 14,
        out_specs=[pl.BlockSpec(memory_space=VMEM)] * 2,
        scratch_shapes=scratch,
        compiler_params=pltpu.CompilerParams(vmem_limit_bytes=56 * 2**20),
        name="compute",
    )(features, cotangent, *halo, w_qkv, w_proj, w_fc1, w_fc2, w_conv, g1, g2, table)


SIDE = 4
HALF_ROWS = GROWS // 2
PART = HALF_ROWS // 3
SHARE = PART // SIDE


def exchange_out(
    d_ref, grads_ref, sum_ref, hr_ref, hs_ref, hc_ref,
    mine, core_in, held, first_in, second_in, third_in,
    halo_send, halo_recv, core_send, core_recv, send, recv,
):
    row, col = lax.axis_index("row"), lax.axis_index("col")
    n_row, n_col = lax.axis_size("row"), lax.axis_size("col")
    up, down = lax.rem(row + n_row - 1, n_row), lax.rem(row + 1, n_row)
    left, right = lax.rem(col + n_col - 1, n_col), lax.rem(col + 1, n_col)
    core, z, y = lax.rem(row, 2), lax.rem(row // 2, SIDE), lax.rem(col, SIDE)
    x = (row // 8) * 2 + col // SIDE
    here = (x, y, z)

    def device(xyz, c):
        return ((xyz[0] // 2) * 8 + xyz[2] * 2 + c, lax.rem(xyz[0], 2) * SIDE + xyz[1])

    def along(axis, k):
        there = list(here)
        there[axis] = lax.rem(there[axis] + k, SIDE)
        return device(there, core)

    sibling = device(here, 1 - core)
    barrier = pltpu.get_barrier_semaphore()
    greeted = [sibling, (up, col), (row, left), (up, left)]
    greeted += [along(axis, k) for axis in range(3) for k in range(1, SIDE)]
    for peer in greeted:
        pl.semaphore_signal(barrier, inc=1, device_id=peer, device_id_type=MESH)
    pl.semaphore_wait(barrier, len(greeted))

    started = []

    def copy(src, dst, s, r, peer):
        c = pltpu.make_async_remote_copy(
            src_ref=src, dst_ref=dst, send_sem=s, recv_sem=r, device_id=peer, device_id_type=MESH
        )
        c.start()
        started.append(c)
        return c

    def rows(start, size):
        return pl.ds(pl.multiple_of(start, 16), size)

    mine_at, other_at = core * HALF_ROWS, (1 - core) * HALF_ROWS
    cores = [
        copy(
            grads_ref.at[rows(other_at + p * PART, PART)],
            core_in.at[p],
            core_send.at[p],
            core_recv.at[p],
            sibling,
        )
        for p in range(3)
    ]
    halos = [copy(d_ref.at[:, 448:512, :], hr_ref, halo_send.at[0], halo_recv.at[0], (down, col))]
    wide = d_ref[NBLK - 1].astype(F32).reshape(ROWS, 2, 8, C)[:, 1]
    mine[...] = low(wide.reshape(ROWS * 8, C))
    halos.append(copy(mine, hs_ref, halo_send.at[1], halo_recv.at[1], (row, right)))
    halos.append(
        copy(mine.at[224:256], hc_ref, halo_send.at[2], halo_recv.at[2], (down, right))
    )

    def spread_out(p, step, source, target, axis):
        target[p, here[axis]] = source
        return [
            copy(
                target.at[p, here[axis]],
                target.at[p, here[axis]],
                send.at[step, p, k - 1],
                recv.at[step, p, k - 1],
                along(axis, k),
            )
            for k in range(1, SIDE)
        ]

    def gathered(copies, target, p):
        for c in copies:
            c.wait_recv()
        total = target[p, 0].astype(F32)
        for k in range(1, SIDE):
            total = total + target[p, k].astype(F32)
        return low(total)

    waits = []
    for p in range(3):
        cores[p].wait_recv()
        own = grads_ref[rows(mine_at + p * PART, PART), :].astype(F32)
        held[p] = low(own + core_in[p].astype(F32))
        group = []
        for k in range(1, SIDE):
            share = lax.rem(here[p] + k, SIDE)
            group.append(
                copy(
                    held.at[p, rows(share * SHARE, SHARE)],
                    first_in.at[p, k - 1],
                    send.at[0, p, k - 1],
                    recv.at[0, p, k - 1],
                    along(p, k),
                )
            )
        waits.append(group)
    nexts = []
    for p in range(3):
        total = held[p, rows(here[p] * SHARE, SHARE), :].astype(F32)
        for k in range(1, SIDE):
            waits[p][k - 1].wait_recv()
            total = total + first_in[p, k - 1].astype(F32)
        nexts.append(spread_out(p, 1, low(total), second_in, (p + 1) % 3))
    lasts = []
    for p in range(3):
        lasts.append(
            spread_out(p, 2, gathered(nexts[p], second_in, p), third_in, (p + 2) % 3)
        )
    backs = []
    for p in range(3):
        at = rows(mine_at + p * PART + here[p] * SHARE, SHARE)
        sum_ref[at, :] = gathered(lasts[p], third_in, p)
        backs.append(
            [
                copy(
                    sum_ref.at[at],
                    sum_ref.at[at],
                    send.at[3, p, k - 1],
                    recv.at[3, p, k - 1],
                    along(p, k),
                )
                for k in range(1, SIDE)
            ]
        )
    ends = []
    for p in range(3):
        for c in backs[p]:
            c.wait_recv()
        at = rows(mine_at + p * PART, PART)
        ends.append(
            copy(sum_ref.at[at], sum_ref.at[at], core_send.at[3 + p], core_recv.at[3 + p], sibling)
        )
    for c in ends + halos:
        c.wait_recv()
    for c in started:
        c.wait_send()


def call_exchange_out(d_shifted, grads):
    slots = VMEM((3, SIDE, SHARE, 128), BF)
    return pl.pallas_call(
        exchange_out,
        out_shape=(
            jax.ShapeDtypeStruct((GROWS, 128), BF),
            jax.ShapeDtypeStruct((NBLK, 64, C), BF),
            jax.ShapeDtypeStruct((256, C), BF),
            jax.ShapeDtypeStruct((32, C), BF),
        ),
        in_specs=[pl.BlockSpec(memory_space=VMEM)] * 2,
        out_specs=[pl.BlockSpec(memory_space=VMEM)] * 4,
        scratch_shapes=[
            VMEM((256, C), BF),
            VMEM((3, PART, 128), BF),
            VMEM((3, PART, 128), BF),
            VMEM((3, SIDE - 1, SHARE, 128), BF),
            slots,
            slots,
            pltpu.SemaphoreType.DMA((3,)),
            pltpu.SemaphoreType.DMA((3,)),
            pltpu.SemaphoreType.DMA((6,)),
            pltpu.SemaphoreType.DMA((6,)),
            pltpu.SemaphoreType.DMA((4, 3, SIDE - 1)),
            pltpu.SemaphoreType.DMA((4, 3, SIDE - 1)),
        ],
        compiler_params=pltpu.CompilerParams(
            collective_id=1, has_side_effects=True, vmem_limit_bytes=32 * 2**20
        ),
        name="exchange_out",
    )(d_shifted, grads)


def results(
    d_ref, hr_ref, hs_ref, hc_ref, sum_ref, out_ref, qkv_ref, proj_ref, fc1_ref, fc2_ref, conv_ref
):
    sub = iota((8, C), 0)
    extras = hs_ref[...].astype(F32).reshape(ROWS, 8, C)
    corners = hc_ref[...].astype(F32).reshape(4, 8, C)
    for i in range(ROWS):
        if i < 4:
            pieces = [hr_ref[b, i * BLK : (i + 1) * BLK, :] for b in range(NBLK)]
            extra = corners[i]
        else:
            pieces = [d_ref[b, (i - 4) * BLK : (i - 3) * BLK, :] for b in range(NBLK)]
            extra = extras[i - 4]
        v = pltpu.roll(jnp.concatenate(pieces, axis=0).astype(F32), 4, 0)
        head = jnp.where(sub < 4, pltpu.roll(extra, 4, 0), v[:8])
        out_ref[i] = low(jnp.concatenate([head, v[8:]], axis=0))

    scale = 1.0 / math.sqrt(ROWS * COLS * lax.axis_size("row") * lax.axis_size("col"))

    def full(i):
        return sum_ref[i * CP : (i + 1) * CP, :]

    def rest(i):
        return full(FULL + i // 2)[:, 64 * (i % 2) : 64 * (i % 2) + 64]

    def square(i, r):
        return jnp.concatenate([full(i), rest(r)], axis=1)

    for t in range(9):
        conv_ref[t] = square(t, t).astype(F32)[:C, :C] * scale
    proj_ref[...] = nn(spread(CP, C, 1), square(9, 9))[:, :C] * scale
    fc2_ref[:CP, :] = square(10, 10).astype(F32)[:, :C] * scale
    fc2_ref[CP:, :] = square(11, 11).astype(F32)[: FF - CP, :C] * scale
    fc1 = jnp.concatenate([full(12), full(13), full(14)], axis=1).astype(F32)
    fc1_ref[...] = fc1[:C, :FF] * scale
    qkv = jnp.concatenate([full(15), full(16), full(17), full(18), rest(12)], axis=1)
    qkv_ref[...] = nn(qkv, spread(3 * CP, 3 * C, 0))[:C] * scale


def call_results(d_shifted, halo, sums):
    return pl.pallas_call(
        results,
        out_shape=(
            jax.ShapeDtypeStruct((ROWS, COLS, C), BF),
            jax.ShapeDtypeStruct((C, 3 * C), F32),
            jax.ShapeDtypeStruct((C, C), F32),
            jax.ShapeDtypeStruct((C, FF), F32),
            jax.ShapeDtypeStruct((FF, C), F32),
            jax.ShapeDtypeStruct((9, C, C), F32),
        ),
        in_specs=[pl.BlockSpec(memory_space=VMEM)] * 5,
        out_specs=[pl.BlockSpec(memory_space=VMEM)] * 6,
        compiler_params=pltpu.CompilerParams(vmem_limit_bytes=32 * 2**20),
        name="results",
    )(d_shifted, *halo, sums)


def bias_rows(pos_table):
    square = pos_table.reshape(15, 15, HEADS)
    rows = jnp.stack([square[:, 7 - kc : 15 - kc] for kc in range(WIN)])
    rows = rows.transpose(3, 0, 1, 2)[:, :, :, None, :]
    return jnp.broadcast_to(rows, (HEADS, WIN, 15, 2, WIN)).reshape(HEADS, WIN, 15 * BLK)


def local(features, cotangent, w_qkv, w_proj, w_fc1, w_fc2, w_conv, gain_attn, gain_mlp, pos_table):
    halo = call_exchange_in(features, cotangent)
    d_shifted, grads = call_compute(
        features,
        cotangent,
        halo,
        w_qkv,
        w_proj,
        w_fc1,
        w_fc2,
        w_conv,
        gain_attn.reshape(1, C),
        gain_mlp.reshape(1, C),
        bias_rows(pos_table),
    )
    sums, *halo_out = call_exchange_out(d_shifted, grads)
    return call_results(d_shifted, halo_out, sums)


def solution(mesh):
    return jax.shard_map(
        local,
        mesh=mesh,
        in_specs=(P("row", "col", None), P("row", "col", None)) + (P(),) * 8,
        out_specs=(P("row", "col", None),) + (P(),) * 5,
        check_vma=False,
    )
```

profile of v0, /device:TPU:1, one launch (start us, length us, event | category | flops | bytes accessed | tf_op | source)
XLA Modules:
  0.0 113.3 jit_solution(1698258356785457751)
XLA Ops:
  0.6 0.8 reshape.27
  1.4 1.7 %copy.20.w2_ref = bf16[360,180]{1,0:T(8,128)(2,1)} copy(bf16[360,180]{0,1:T(8,128)(2,1)} %param.15) | data formatting | bytes 259200 | tf_op args[5]
  3.1 0.1 fusion.7
  3.2 0.1 fusion.6
  3.3 0.1 fusion.5
  3.4 0.1 fusion.4
  3.4 0.1 fusion.3
  3.5 0.1 fusion.2
  3.6 0.1 fusion.1
  3.7 0.0 copy-start
  3.7 0.0 copy-start.1
  3.8 0.3 broadcast_in_dim.2
  4.0 1.1 reshape.28.d_ref
  5.2 0.0 copy-done
  5.2 0.1 copy-done.1
  5.3 11.9 %exchange_in.1 = (bf16[4,64,180]{2,1,0:T(8,128)(2,1)S(1)}, bf16[5,64,180]{2,1,0:T(8,128)(2,1)S(1)}, bf16[288,180]{1,0:T(8,128)(2,1)S(1)}, bf16[80,180]{1,0:T(8,128)(2,1)S(1)}) custom-call(bf16[32,64,180]{2,1,0:T(8,128)(2,1)S(1)} %copy-done, bf16[32,64,180]{2,1,0:T(8,128)(2,1)S(1)} %copy-done.1), custom_call_target="tpu_custom_call" | custom-call | tf_op jit(solution)/shard_map/exchange_in/pallas_call | solution.py:99
  17.2 0.0 copy-start.4
  17.2 0.7 copy-done.4
  17.8 0.0 copy-start.5
  17.8 0.7 copy-done.5
  18.5 0.0 copy-start.6
  18.5 0.7 copy-done.6
  19.1 0.0 copy-start.7
  19.1 0.6 copy-done.7
  19.8 54.5 %compute.1 = (bf16[4,512,180]{2,1,0:T(8,128)(2,1)}, bf16[4992,128]{1,0:T(8,128)(2,1)}) custom-call(bf16[32,64,180]{2,1,0:T(8,128)(2,1)} %f_ref.3, bf16[32,64,180]{2,1,0:T(8,128)(2,1)} %g_ref.3, bf16[4,64,180]{2,1,0:T(8,128)(2,1)} %copy-done.6, bf16[5,64,180]{2,1,0:T(8,128)(2,1)} %copy-done.4, bf16[288,180]{1,0:T(8,128)(2,1)} %copy-done.5, ...), custom_call_target="tpu_custom_call" | custom-call | tf_op jit(solution)/shard_map/compute/pallas_call | solution.py:422
  74.2 0.0 copy-start.2
  74.2 1.2 %copy-done.2 = bf16[4,512,180]{2,1,0:T(8,128)(2,1)S(1)} copy-done((bf16[4,512,180]{2,1,0:T(8,128)(2,1)S(1)}, bf16[4,512,180]{2,1,0:T(8,128)(2,1)}, u32[]{:S(2)}) %copy-start.2) | copy-done | bytes 737304
  75.4 0.0 copy-start.3
  75.4 1.3 %copy-done.3 = bf16[4992,128]{1,0:T(8,128)(2,1)S(1)} copy-done((bf16[4992,128]{1,0:T(8,128)(2,1)S(1)}, bf16[4992,128]{1,0:T(8,128)(2,1)}, u32[]{:S(2)}) %copy-start.3) | copy-done | bytes 1277976
  76.7 33.4 %exchange_out.1 = (bf16[4992,128]{1,0:T(8,128)(2,1)S(1)}, bf16[4,64,180]{2,1,0:T(8,128)(2,1)S(1)}, bf16[256,180]{1,0:T(8,128)(2,1)S(1)}, bf16[32,180]{1,0:T(8,128)(2,1)S(1)}) custom-call(bf16[4,512,180]{2,1,0:T(8,128)(2,1)S(1)} %copy-done.2, bf16[4992,128]{1,0:T(8,128)(2,1)S(1)} %copy-done.3), custom_call_target="tpu_custom_call" | custom-call | tf_op jit(solution)/shard_map/exchange_out/pallas_call | solution.py:586
  110.1 2.3 %results.1 = (bf16[32,64,180]{2,1,0:T(8,128)(2,1)}, f32[180,540]{1,0:T(8,128)}, f32[180,180]{1,0:T(8,128)}, f32[180,360]{1,0:T(8,128)}, f32[360,180]{1,0:T(8,128)S(1)}, /*index=5*/f32[9,180,180]{2,1,0:T(8,128)}) custom-call(bf16[4,512,180]{2,1,0:T(8,128)(2,1)S(1)} %copy-done.2, bf16[4,64,180]{2,1,0:T(8,128)(2,1)S(1)} %get-tuple-element.22.hr_ref, ...), custom_call_target="tpu_custom_call" | custom-call | tf_op jit(solution)/shard_map/results/pallas_call | solution.py:657
  112.5 0.9 copy.21
  (2 shorter events, 0.0 us)
Async XLA Ops:
  3.7 1.4 %copy-start = (bf16[32,64,180]{2,1,0:T(8,128)(2,1)S(1)}, bf16[32,64,180]{2,1,0:T(8,128)(2,1)}, u32[]{:S(2)}) copy-start(bf16[32,64,180]{2,1,0:T(8,128)(2,1)} %f_ref.3) | copy-start | bytes 2211844
  3.7 1.5 %copy-start.1 = (bf16[32,64,180]{2,1,0:T(8,128)(2,1)S(1)}, bf16[32,64,180]{2,1,0:T(8,128)(2,1)}, u32[]{:S(2)}) copy-start(bf16[32,64,180]{2,1,0:T(8,128)(2,1)} %g_ref.3) | copy-start | bytes 2211844
  17.2 0.7 copy-start.4
  17.8 0.7 copy-start.5
  18.5 0.7 copy-start.6
  19.1 0.6 copy-start.7
  74.2 1.2 %copy-start.2 = (bf16[4,512,180]{2,1,0:T(8,128)(2,1)S(1)}, bf16[4,512,180]{2,1,0:T(8,128)(2,1)}, u32[]{:S(2)}) copy-start(bf16[4,512,180]{2,1,0:T(8,128)(2,1)} %get-tuple-element.20.d_ref) | copy-start | bytes 2211844
  75.4 1.3 %copy-start.3 = (bf16[4992,128]{1,0:T(8,128)(2,1)S(1)}, bf16[4992,128]{1,0:T(8,128)(2,1)}, u32[]{:S(2)}) copy-start(bf16[4992,128]{1,0:T(8,128)(2,1)} %get-tuple-element.21.grads_ref) | copy-start | bytes 3833860
where the time goes:
time: 114 us; the launch traced here: 113 us
  Pallas kernels  102 us (89%)
  local copies, waits for them, and re-layouts  10.5 us (9%)
    pallas_call x1, Pallas kernels, call_compute(): pl.pallas_call(compute, out_shape=(jax.ShapeDtypeStruct((NBLK, TOK, C), B...  54.5 us
    pallas_call x1, Pallas kernels, call_exchange_out(): pl.pallas_call(exchange_out, out_shape=(jax.ShapeDtypeStruct((GROWS, 128)...  33.4 us
    pallas_call x1, Pallas kernels, call_exchange_in(): pl.pallas_call(exchange_in, out_shape=(jax.ShapeDtypeStruct((4, COLS, C),...  11.9 us
    unnamed x24, local copies, waits for them, and re-layouts  7.5 us
    pallas_call x1, Pallas kernels, call_results(): pl.pallas_call(results, out_shape=(jax.ShapeDtypeStruct((ROWS, COLS, C),...  2.33 us

commit v1 on v0

v1 whole, which is shorter than its diff:
```python
import math

import jax
import jax.numpy as jnp
from jax import lax
from jax.experimental import pallas as pl
from jax.experimental.pallas import tpu as pltpu
from jax.sharding import PartitionSpec as P

C = 180
CP = 192
HEADS = 6
HD = 30
HP = 32
FF = 360
WIN = 8
SHIFT = 4
ROWS = 32
COLS = 64
BLK = 16
NBLK = COLS // BLK
TOK = ROWS * BLK
PAIR = WIN * BLK
SIDE = 4
TILES = (22, 6)
BASE = (0, TILES[0] * CP)
GROWS = sum(TILES) * CP
HALVES = tuple(t * CP // 2 for t in TILES)
PARTS = tuple(h // 3 for h in HALVES)
SHARES = tuple(p // SIDE for p in PARTS)
BF = jnp.bfloat16
F32 = jnp.float32
MESH = pl.DeviceIdType.MESH
VMEM = pltpu.VMEM


def iota(shape, dim):
    return lax.broadcasted_iota(jnp.int32, shape, dim)


def nn(a, b):
    return lax.dot_general(a, b, (((1,), (0,)), ((), ())), preferred_element_type=F32)


def nt(a, b):
    return lax.dot_general(a, b, (((1,), (1,)), ((), ())), preferred_element_type=F32)


def low(a):
    return a.astype(BF)


def eye(rows, cols):
    return low(jnp.where(iota((rows, cols), 0) == iota((rows, cols), 1), 1.0, 0.0))


def spread(padded, plain, pad_dim):
    shape = (padded, plain) if pad_dim == 0 else (plain, padded)
    p = iota(shape, pad_dim)
    c = iota(shape, 1 - pad_dim)
    hit = ((p & (HP - 1)) < HD) & (c == (p >> 5) * HD + (p & (HP - 1)))
    return low(jnp.where(hit, 1.0, 0.0))


def column(gain_ref):
    wide = jnp.where(iota((CP, C), 0) == iota((CP, C), 1), gain_ref[...], 0.0)
    return jnp.sum(wide, axis=1, keepdims=True)


def moments(values):
    mean = jnp.sum(values[:C], axis=0, keepdims=True) * (1.0 / C)
    centred = values - mean
    inner = centred[:C]
    var = jnp.sum(inner * inner, axis=0, keepdims=True) * (1.0 / C)
    return centred, lax.rsqrt(var + 1e-05)


def norm_back(upstream, normed, inverse, gain):
    scaled = upstream * gain
    first = jnp.sum(scaled, axis=0, keepdims=True) * (1.0 / C)
    second = jnp.sum(scaled * normed, axis=0, keepdims=True) * (1.0 / C)
    return inverse * (scaled - first - normed * second)


def gelu_parts(x):
    u = jnp.abs(x) * math.sqrt(0.5)
    t = 1.0 / (1.0 + 0.3275911 * u)
    e = jnp.exp(-u * u)
    poly = t * (
        0.254829592
        + t * (-0.284496736 + t * (1.421413741 + t * (-1.453152027 + t * 1.061405429)))
    )
    tail = 0.5 * poly * e
    cdf = jnp.where(x >= 0.0, 1.0 - tail, tail)
    return cdf, e * (1.0 / math.sqrt(2.0 * math.pi))


def fold(scores, second):
    parts = scores.reshape(WIN, 2, WIN, PAIR)
    return jnp.where(second, parts[:, 1], parts[:, 0]).reshape(WIN * WIN, PAIR)


def unfold(probs, second):
    parts = probs.reshape(WIN, WIN, PAIR)
    zero = jnp.zeros_like(parts)
    both = jnp.stack([jnp.where(second, zero, parts), jnp.where(second, parts, zero)], axis=1)
    return low(both.reshape(PAIR, PAIR))


def two_heads(block):
    zero = jnp.zeros((HP, PAIR), BF)
    top = jnp.concatenate([block[:HP], zero], axis=1)
    return jnp.concatenate([top, jnp.concatenate([zero, block[HP:]], axis=1)], axis=0)


def own_heads(product):
    return jnp.concatenate([product[:HP, :PAIR], product[HP:, PAIR:]], axis=0)


def tn(a, b):
    return lax.dot_general(a, b, (((0,), (0,)), ((), ())), preferred_element_type=F32)


def layer(
    f_ref, g_ref, wqkv_ref, wproj_ref, w1_ref, w2_ref, wconv_ref, g1_ref, g2_ref, pos_ref,
    d_ref, sum_ref, hr_ref, hs_ref, hc_ref,
    fr_ref, gr_ref, strip_ref, corner_ref, strip_in, strip_out,
    grads_ref, core_in0, core_in1, held0, held1, first0, first1, second0, second1, third0, third1,
    xs, gs, wqkvt, wqkvp, wprojt, wprojp, w1t, w1p, w2t, w2p, wcp, bias,
    s_x, s_inv1, s_n1, packed, attended, probs, s_norm2, s_inv2, s_n2, s_slope, s_hidden, s_z,
    dheads, dpacked, s_dmid,
    a_conv, a_proj, a_fc1, a_fc2, a_qkv,
    in_send, in_recv, out_send, out_recv, core_send, core_recv, send, recv,
):
    row, col = lax.axis_index("row"), lax.axis_index("col")
    n_row, n_col = lax.axis_size("row"), lax.axis_size("col")
    up, down = lax.rem(row + n_row - 1, n_row), lax.rem(row + 1, n_row)
    left, right = lax.rem(col + n_col - 1, n_col), lax.rem(col + 1, n_col)
    last_row, last_col = row == n_row - 1, col == n_col - 1
    factor = HD**-0.5
    core, z, y = lax.rem(row, 2), lax.rem(row // 2, SIDE), lax.rem(col, SIDE)
    x = (row // 8) * 2 + col // SIDE
    here = (x, y, z)

    def device(xyz, c):
        return ((xyz[0] // 2) * 8 + xyz[2] * 2 + c, lax.rem(xyz[0], 2) * SIDE + xyz[1])

    def along(axis, k):
        there = list(here)
        there[axis] = lax.rem(there[axis] + k, SIDE)
        return device(there, core)

    sibling = device(here, 1 - core)
    barrier = pltpu.get_barrier_semaphore()
    greeted = [sibling, (up, col), (row, left), (up, left), (down, col), (row, right)]
    greeted += [(down, right)] + [along(axis, k) for axis in range(3) for k in range(1, SIDE)]
    for peer in greeted:
        pl.semaphore_signal(barrier, inc=1, device_id=peer, device_id_type=MESH)

    started = []

    def copy(src, dst, s, r, peer):
        c = pltpu.make_async_remote_copy(
            src_ref=src, dst_ref=dst, send_sem=s, recv_sem=r, device_id=peer, device_id_type=MESH
        )
        c.start()
        started.append(c)
        return c

    fs = f_ref[:, 0:16, :].astype(F32)[:, 0:8, :]
    cs = g_ref[:, 0:16, :].astype(F32)[:, 0:8, :]
    both = jnp.where(iota((ROWS, 8, C), 1) < 4, fs, pltpu.roll(cs, 4, 1))
    strip_in[32:288, :] = low(both.reshape(ROWS * 8, C))
    strip_in[0:32, :] = low(cs[:, 4, :])
    pl.semaphore_wait(barrier, len(greeted))
    arriving = [
        copy(strip_in.at[0:80], corner_ref, in_send.at[3], in_recv.at[3], (up, left)),
        copy(strip_in, strip_ref, in_send.at[2], in_recv.at[2], (row, left)),
        copy(f_ref.at[0:4], fr_ref, in_send.at[0], in_recv.at[0], (up, col)),
        copy(g_ref.at[0:5], gr_ref, in_send.at[1], in_recv.at[1], (up, col)),
    ]

    pad = eye(CP, C)
    sel, sel_one = spread(3 * CP, 3 * C, 0), spread(CP, C, 0)
    wq = low(nn(pad, wqkv_ref[...]))
    wqkvt[...] = low(nt(sel, wq))
    wqkvp[...] = low(nt(wq, sel))
    turned = low(nt(pad, wproj_ref[...]))
    wprojt[...] = low(nt(turned, sel_one))
    wprojp[...] = low(nt(sel_one, turned))
    w1p[...] = low(nn(pad, w1_ref[...]))
    w1t[...] = low(nt(eye(FF, FF), w1p[...]))
    w2t[...] = low(nn(pad, w2_ref[...]))
    w2p[...] = low(nt(eye(FF, FF), w2t[...]))
    for t in range(9):
        wcp[t] = low(nn(pad, wconv_ref[t]))
    gain1, gain2 = column(g1_ref), column(g2_ref)

    table = pos_ref[...]
    high = low(table)
    mid = low(table - high.astype(F32))
    rest_piece = low(table - high.astype(F32) - mid.astype(F32))
    entry, place = iota((225, 15 * BLK), 0), iota((225, 15 * BLK), 1)
    for kc in range(WIN):
        hit = entry == (place >> 4) * 15 + (place & 7) - kc + 7
        pick = low(jnp.where(hit, 1.0, 0.0))
        line = nn(high, pick) + nn(mid, pick) + nn(rest_piece, pick)
        for h in range(HEADS):
            for kr in range(WIN):
                start = (WIN - 1 - kr) * BLK
                at = kr * WIN + kc
                bias[h, at : at + 1, :] = line[h : h + 1, start : start + PAIR]
    for acc in (a_conv, a_proj, a_fc1, a_fc2, a_qkv):
        acc[...] = jnp.zeros_like(acc)

    for c in arriving:
        c.wait_recv()

    sub = iota((8, C), 0)

    def tail(body, last):
        return jnp.concatenate([body[:56], last], axis=0)

    def put_x(i, v, extra):
        rolled = pltpu.roll(v, 60, 0)
        whole = low(tail(rolled, jnp.where(sub < 4, rolled[56:], pltpu.roll(extra, 4, 0))))
        for b in range(NBLK):
            xs[b, i * BLK : (i + 1) * BLK, :] = whole[b * BLK : (b + 1) * BLK]

    keep0 = jnp.where((sub == 3) & last_col, 0.0, 1.0)
    keep2 = jnp.where((sub == 4) & last_col, 0.0, 1.0)

    def put_g(i, v, extra, fifth):
        r5, r4, r3 = pltpu.roll(v, 59, 0), pltpu.roll(v, 60, 0), pltpu.roll(v, 61, 0)
        e5 = jnp.where(sub == 7, fifth, pltpu.roll(extra, 7, 0))
        l5 = jnp.where(sub < 3, r5[56:], e5) * keep0
        l4 = jnp.where(sub < 4, r4[56:], extra)
        l3 = jnp.where(sub < 5, r3[56:], pltpu.roll(extra, 1, 0)) * keep2
        for k, (r, last) in enumerate(((r5, l5), (r4, l4), (r3, l3))):
            whole = low(tail(r, last))
            for b in range(NBLK):
                gs[k, b, i * BLK : (i + 1) * BLK, :] = whole[b * BLK : (b + 1) * BLK]

    extras = strip_ref[32:288, :].astype(F32).reshape(ROWS, 8, C)
    fifths = strip_ref[0:32, :].astype(F32)
    c_extras = corner_ref[32:80, :].astype(F32).reshape(6, 8, C)
    c_fifths = corner_ref[0:16, :].astype(F32)
    for i in range(ROWS):
        if i < ROWS - 4:
            put_x(i, f_ref[i + 4].astype(F32), extras[i + 4])
        else:
            put_x(i, fr_ref[i - 28].astype(F32), c_extras[i - 28])
    for i in range(ROWS + 2):
        if i < ROWS - 3:
            put_g(i, g_ref[i + 3].astype(F32), extras[i + 3], fifths[i + 3 : i + 4])
        else:
            k = i - 29
            put_g(i, gr_ref[k].astype(F32), c_extras[k], c_fifths[k : k + 1])

    lane = iota((1, PAIR), 1)
    second = ((lane >> 3) & 1) == 1
    k_sub, q_lane = iota((WIN * WIN, PAIR), 0), iota((WIN * WIN, PAIR), 1)
    rows_differ = ((k_sub >> 5) & 1) != ((q_lane >> 6) & 1)
    cols_differ = (((k_sub >> 2) & 1) != ((q_lane >> 2) & 1)) & (((q_lane >> 3) & 1) == 1)
    tok = iota((1, TOK), 1) >> 4
    drop0 = (tok == 27) & last_row
    drop2 = (tok == 28) & last_row

    def forward(b, carry):
        x = nt(pad, xs[b])
        centred, inv1 = moments(x)
        normed1 = centred * inv1
        s_x[b] = normed1
        s_inv1[b] = inv1
        n1 = low(normed1 * gain1)
        s_n1[b] = n1
        packed[b] = low(nn(wqkvt[...], n1))
        col_flag = last_col & (b == NBLK - 1)

        def attend(a, carry):
            lanes = pl.ds(pl.multiple_of(a * PAIR, PAIR), PAIR)
            row_flag = last_row & (a == ROWS // WIN - 1)
            mask = jnp.where((rows_differ & row_flag) | (cols_differ & col_flag), -100.0, 0.0)
            for j in range(HEADS // 2):
                q = packed[b, 64 * j : 64 * j + 64, lanes]
                k = packed[b, CP + 64 * j : CP + 64 * j + 64, lanes]
                v = packed[b, 2 * CP + 64 * j : 2 * CP + 64 * j + 64, lanes]
                scores = tn(k, two_heads(q))
                wide = []
                for s in range(2):
                    sc = fold(scores[:, s * PAIR : (s + 1) * PAIR], second)
                    sc = sc * factor + bias[2 * j + s] + mask
                    e = jnp.exp(sc - jnp.max(sc, axis=0, keepdims=True))
                    p = e * (1.0 / jnp.sum(e, axis=0, keepdims=True))
                    probs[b, a, 2 * j + s] = p
                    wide.append(unfold(p, second))
                o = nn(v, jnp.concatenate(wide, axis=1))
                attended[b, 64 * j : 64 * j + 64, lanes] = low(own_heads(o))
            return carry

        lax.fori_loop(0, ROWS // WIN, attend, 0, unroll=True)

        middle = x + nn(wprojt[...], attended[b])
        centred2, inv2 = moments(middle)
        normed2 = centred2 * inv2
        s_norm2[b] = normed2
        s_inv2[b] = inv2
        n2 = low(normed2 * gain2)
        s_n2[b] = n2
        pre = nn(w1t[...], n2)
        cdf, pdf = gelu_parts(pre)
        hidden = low(pre * cdf)
        s_hidden[b] = hidden
        s_slope[b] = cdf + pre * pdf
        s_z[b] = low(middle + nn(w2t[...], hidden))
        return carry

    lax.fori_loop(0, NBLK, forward, 0)

    def back_to_heads(b, carry):
        z = s_z[b]
        z0 = jnp.where(drop0, 0.0, z.astype(F32)).astype(BF)
        z2 = jnp.where(drop2, 0.0, z.astype(F32)).astype(BF)
        total = jnp.zeros((CP, TOK), F32)
        for dy in range(3):
            part = jnp.zeros((CP, TOK), F32)
            zd = (z0, z, z2)[dy]
            for dx in range(3):
                source = gs[dx, b, (2 - dy) * BLK : (2 - dy) * BLK + TOK, :]
                part = part + nt(wcp[3 * dy + dx], source)
                a_conv[3 * dy + dx] += nn(zd, source)
            if dy == 0:
                part = jnp.where(drop0, 0.0, part)
            if dy == 2:
                part = jnp.where(drop2, 0.0, part)
            total = total + part
        d_shift = low(total)
        a_fc2[:, :FF] += nt(d_shift, s_hidden[b])
        d_pre = low(nn(w2p[...], d_shift) * s_slope[b])
        a_fc1[:, :FF] += nt(s_n2[b], d_pre)
        d_middle = d_shift.astype(F32) + norm_back(
            nn(w1p[...], d_pre), s_norm2[b], s_inv2[b], gain2
        )
        s_dmid[b] = d_middle
        d_attn = low(d_middle)
        a_proj[...] += nt(attended[b], d_attn)
        dheads[b] = low(nn(wprojp[...], d_attn))
        return carry

    lax.fori_loop(0, NBLK, back_to_heads, 0)

    steps = (
        (core_in0, held0, first0, second0, third0),
        (core_in1, held1, first1, second1, third1),
    )
    flying = [{}, {}]

    def rows(start, size):
        return pl.ds(pl.multiple_of(start, 16), size)

    def at_part(g, c, p):
        return BASE[g] + c * HALVES[g] + p * PARTS[g]

    def go_core(g):
        flying[g]["core"] = [
            copy(
                grads_ref.at[rows(at_part(g, 1 - core, p), PARTS[g])],
                steps[g][0].at[p],
                core_send.at[g, p],
                core_recv.at[g, p],
                sibling,
            )
            for p in range(3)
        ]

    def go_first(g):
        core_in, held, first = steps[g][:3]
        flying[g]["first"] = []
        for p in range(3):
            flying[g]["core"][p].wait_recv()
            own = grads_ref[rows(at_part(g, core, p), PARTS[g]), :].astype(F32)
            held[p] = low(own + core_in[p].astype(F32))
            group = []
            for k in range(1, SIDE):
                share = lax.rem(here[p] + k, SIDE)
                group.append(
                    copy(
                        held.at[p, rows(share * SHARES[g], SHARES[g])],
                        first.at[p, k - 1],
                        send.at[g, 0, p, k - 1],
                        recv.at[g, 0, p, k - 1],
                        along(p, k),
                    )
                )
            flying[g]["first"].append(group)

    def spread_out(g, p, step, source, target, axis):
        target[p, here[axis]] = source
        return [
            copy(
                target.at[p, here[axis]],
                target.at[p, here[axis]],
                send.at[g, step, p, k - 1],
                recv.at[g, step, p, k - 1],
                along(axis, k),
            )
            for k in range(1, SIDE)
        ]

    def gathered(copies, target, p):
        for c in copies:
            c.wait_recv()
        total = target[p, 0].astype(F32)
        for k in range(1, SIDE):
            total = total + target[p, k].astype(F32)
        return low(total)

    def go_second(g):
        held, first, second_in = steps[g][1:4]
        flying[g]["second"] = []
        for p in range(3):
            total = held[p, rows(here[p] * SHARES[g], SHARES[g]), :].astype(F32)
            for k in range(1, SIDE):
                flying[g]["first"][p][k - 1].wait_recv()
                total = total + first[p, k - 1].astype(F32)
            flying[g]["second"].append(
                spread_out(g, p, 1, low(total), second_in, (p + 1) % 3)
            )

    def go_third(g):
        second_in, third_in = steps[g][3:5]
        flying[g]["third"] = []
        for p in range(3):
            total = gathered(flying[g]["second"][p], second_in, p)
            flying[g]["third"].append(spread_out(g, p, 2, total, third_in, (p + 2) % 3))

    def go_back(g):
        flying[g]["back"] = []
        for p in range(3):
            at = rows(at_part(g, core, p) + here[p] * SHARES[g], SHARES[g])
            sum_ref[at, :] = gathered(flying[g]["third"][p], steps[g][4], p)
            flying[g]["back"].append(
                [
                    copy(
                        sum_ref.at[at],
                        sum_ref.at[at],
                        send.at[g, 3, p, k - 1],
                        recv.at[g, 3, p, k - 1],
                        along(p, k),
                    )
                    for k in range(1, SIDE)
                ]
            )

    def go_end(g):
        flying[g]["end"] = []
        for p in range(3):
            for c in flying[g]["back"][p]:
                c.wait_recv()
            at = rows(at_part(g, core, p), PARTS[g])
            flying[g]["end"].append(
                copy(
                    sum_ref.at[at],
                    sum_ref.at[at],
                    core_send.at[g, 3 + p],
                    core_recv.at[g, 3 + p],
                    sibling,
                )
            )

    def put(place, tile):
        grads_ref[place * CP : (place + 1) * CP, :] = low(tile)

    half_zero = jnp.zeros((CP, 64), F32)
    rests = []
    for t in range(9):
        put(t, a_conv[t, :, 0:128])
        rests.append(jnp.concatenate([a_conv[t, :, 128:C], half_zero[:, : 64 - (C - 128)]], axis=1))
    put(9, a_proj[:, 0:128])
    rests.append(a_proj[:, 128:192])
    for i in range(3):
        put(10 + i, a_fc2[:, i * 128 : (i + 1) * 128])
        put(13 + i, a_fc1[:, i * 128 : (i + 1) * 128])
    for i in range(5):
        put(16 + i, jnp.concatenate([rests[2 * i], rests[2 * i + 1]], axis=1))
    put(21, jnp.zeros((CP, 128), F32))
    go_core(0)

    def heads_back(b):
        def attend_back(a, carry):
            lanes = pl.ds(pl.multiple_of(a * PAIR, PAIR), PAIR)
            for j in range(HEADS // 2):
                q = packed[b, 64 * j : 64 * j + 64, lanes]
                k = packed[b, CP + 64 * j : CP + 64 * j + 64, lanes]
                v = packed[b, 2 * CP + 64 * j : 2 * CP + 64 * j + 64, lanes]
                do = dheads[b, 64 * j : 64 * j + 64, lanes]
                d_prob = tn(v, two_heads(do))
                p_wide, s_wide = [], []
                for s in range(2):
                    p = probs[b, a, 2 * j + s]
                    dp = fold(d_prob[:, s * PAIR : (s + 1) * PAIR], second)
                    ds = p * (dp - jnp.sum(p * dp, axis=0, keepdims=True)) * factor
                    p_wide.append(unfold(p, second))
                    s_wide.append(unfold(ds, second))
                dv = nt(do, jnp.concatenate(p_wide, axis=0))
                dq = nn(k, jnp.concatenate(s_wide, axis=1))
                dk = nt(q, jnp.concatenate(s_wide, axis=0))
                dpacked[b, 64 * j : 64 * j + 64, lanes] = low(own_heads(dq))
                dpacked[b, CP + 64 * j : CP + 64 * j + 64, lanes] = low(own_heads(dk))
                dpacked[b, 2 * CP + 64 * j : 2 * CP + 64 * j + 64, lanes] = low(own_heads(dv))
            return carry

        lax.fori_loop(0, ROWS // WIN, attend_back, 0, unroll=True)
        a_qkv[...] += nt(s_n1[b], dpacked[b])

    heads_back(0)
    go_first(0)
    heads_back(1)
    go_second(0)
    heads_back(2)
    go_third(0)
    heads_back(3)
    for i in range(4):
        put(22 + i, a_qkv[:, i * 128 : (i + 1) * 128])
    put(26, jnp.concatenate([a_qkv[:, 512:576], half_zero], axis=1))
    put(27, jnp.zeros((CP, 128), F32))
    go_core(1)
    go_back(0)

    ones_pair = eye(PAIR, PAIR)

    def inputs_back(b):
        d_in = s_dmid[b] + norm_back(nn(wqkvp[...], dpacked[b]), s_x[b], s_inv1[b], gain1)
        d_low = low(d_in)
        for a in range(ROWS // WIN):
            natural = nt(ones_pair, d_low[:, a * PAIR : (a + 1) * PAIR])
            d_ref[b, a * PAIR : (a + 1) * PAIR, :] = low(natural[:, :C])

    inputs_back(NBLK - 1)
    go_first(1)
    edge = d_ref[NBLK - 1].astype(F32).reshape(ROWS, 2, 8, C)[:, 1]
    strip_out[...] = low(edge.reshape(ROWS * 8, C))
    leaving = [
        copy(strip_out.at[224:256], hc_ref, out_send.at[2], out_recv.at[2], (down, right)),
        copy(strip_out, hs_ref, out_send.at[1], out_recv.at[1], (row, right)),
    ]
    inputs_back(0)
    inputs_back(1)
    go_second(1)
    inputs_back(2)
    leaving.append(
        copy(d_ref.at[:, 448:512, :], hr_ref, out_send.at[0], out_recv.at[0], (down, col))
    )
    go_end(0)
    go_third(1)
    go_back(1)
    go_end(1)
    for c in flying[0]["end"] + flying[1]["end"] + leaving:
        c.wait_recv()
    for c in started:
        c.wait_send()


def call_layer(features, cotangent, w_qkv, w_proj, w_fc1, w_fc2_t, w_conv, g1, g2, table):
    blocks = ROWS // WIN
    reductions = []
    for sizes in (
        (3, PARTS),
        (3, PARTS),
        ((3, SIDE - 1), SHARES),
        ((3, SIDE), SHARES),
        ((3, SIDE), SHARES),
    ):
        lead, lengths = sizes
        lead = lead if isinstance(lead, tuple) else (lead,)
        reductions += [VMEM((*lead, n, 128), BF) for n in lengths]
    scratch = [
        VMEM((4, COLS, C), BF),
        VMEM((5, COLS, C), BF),
        VMEM((288, C), BF),
        VMEM((80, C), BF),
        VMEM((288, C), BF),
        VMEM((256, C), BF),
        VMEM((GROWS, 128), BF),
        *reductions,
        VMEM((NBLK, TOK, C), BF),
        VMEM((3, NBLK, (ROWS + 2) * BLK, C), BF),
        VMEM((3 * CP, CP), BF),
        VMEM((CP, 3 * CP), BF),
        VMEM((CP, CP), BF),
        VMEM((CP, CP), BF),
        VMEM((FF, CP), BF),
        VMEM((CP, FF), BF),
        VMEM((CP, FF), BF),
        VMEM((FF, CP), BF),
        VMEM((9, CP, C), BF),
        VMEM((HEADS, WIN * WIN, PAIR), F32),
        VMEM((NBLK, CP, TOK), F32),
        VMEM((NBLK, 1, TOK), F32),
        VMEM((NBLK, CP, TOK), BF),
        VMEM((NBLK, 3 * CP, TOK), BF),
        VMEM((NBLK, CP, TOK), BF),
        VMEM((NBLK, blocks, HEADS, WIN * WIN, PAIR), F32),
        VMEM((NBLK, CP, TOK), F32),
        VMEM((NBLK, 1, TOK), F32),
        VMEM((NBLK, CP, TOK), BF),
        VMEM((NBLK, FF, TOK), F32),
        VMEM((NBLK, FF, TOK), BF),
        VMEM((NBLK, CP, TOK), BF),
        VMEM((NBLK, CP, TOK), BF),
        VMEM((NBLK, 3 * CP, TOK), BF),
        VMEM((NBLK, CP, TOK), F32),
        VMEM((9, CP, C), F32),
        VMEM((CP, CP), F32),
        VMEM((CP, 384), F32),
        VMEM((CP, 384), F32),
        VMEM((CP, 3 * CP), F32),
        pltpu.SemaphoreType.DMA((4,)),
        pltpu.SemaphoreType.DMA((4,)),
        pltpu.SemaphoreType.DMA((3,)),
        pltpu.SemaphoreType.DMA((3,)),
        pltpu.SemaphoreType.DMA((2, 6)),
        pltpu.SemaphoreType.DMA((2, 6)),
        pltpu.SemaphoreType.DMA((2, 4, 3, SIDE - 1)),
        pltpu.SemaphoreType.DMA((2, 4, 3, SIDE - 1)),
    ]
    return pl.pallas_call(
        layer,
        out_shape=(
            jax.ShapeDtypeStruct((NBLK, TOK, C), BF),
            jax.ShapeDtypeStruct((GROWS, 128), BF),
            jax.ShapeDtypeStruct((NBLK, 64, C), BF),
            jax.ShapeDtypeStruct((256, C), BF),
            jax.ShapeDtypeStruct((32, C), BF),
        ),
        in_specs=[pl.BlockSpec(memory_space=VMEM)] * 10,
        out_specs=[pl.BlockSpec(memory_space=VMEM)] * 5,
        scratch_shapes=scratch,
        compiler_params=pltpu.CompilerParams(
            collective_id=0, has_side_effects=True, vmem_limit_bytes=60 * 2**20
        ),
        name="layer",
    )(features, cotangent, w_qkv, w_proj, w_fc1, w_fc2_t, w_conv, g1, g2, table)


def results(
    d_ref, hr_ref, hs_ref, hc_ref, sum_ref, out_ref, qkv_ref, proj_ref, fc1_ref, fc2_ref, conv_ref
):
    sub = iota((8, C), 0)
    extras = hs_ref[...].astype(F32).reshape(ROWS, 8, C)
    corners = hc_ref[...].astype(F32).reshape(4, 8, C)
    for i in range(ROWS):
        if i < 4:
            pieces = [hr_ref[b, i * BLK : (i + 1) * BLK, :] for b in range(NBLK)]
            extra = corners[i]
        else:
            pieces = [d_ref[b, (i - 4) * BLK : (i - 3) * BLK, :] for b in range(NBLK)]
            extra = extras[i - 4]
        v = pltpu.roll(jnp.concatenate(pieces, axis=0).astype(F32), 4, 0)
        head = jnp.where(sub < 4, pltpu.roll(extra, 4, 0), v[:8])
        out_ref[i] = low(jnp.concatenate([head, v[8:]], axis=0))

    scale = 1.0 / math.sqrt(ROWS * COLS * lax.axis_size("row") * lax.axis_size("col"))

    def full(i):
        return sum_ref[i * CP : (i + 1) * CP, :]

    def rest(i):
        return full(16 + i // 2)[:, 64 * (i % 2) : 64 * (i % 2) + 64]

    def square(i, r):
        return jnp.concatenate([full(i), rest(r)], axis=1)

    for t in range(9):
        conv_ref[t] = square(t, t).astype(F32)[:C, :C] * scale
    proj_ref[...] = nn(spread(CP, C, 1), square(9, 9))[:, :C] * scale
    fc2 = jnp.concatenate([full(10), full(11), full(12)], axis=1).astype(F32)
    fc2_ref[...] = fc2[:C, :FF] * scale
    fc1 = jnp.concatenate([full(13), full(14), full(15)], axis=1).astype(F32)
    fc1_ref[...] = fc1[:C, :FF] * scale
    qkv = jnp.concatenate([full(22), full(23), full(24), full(25), full(26)[:, :64]], axis=1)
    qkv_ref[...] = nn(qkv, spread(3 * CP, 3 * C, 0))[:C] * scale


def call_results(d_shifted, halo, sums):
    return pl.pallas_call(
        results,
        out_shape=(
            jax.ShapeDtypeStruct((ROWS, COLS, C), BF),
            jax.ShapeDtypeStruct((C, 3 * C), F32),
            jax.ShapeDtypeStruct((C, C), F32),
            jax.ShapeDtypeStruct((C, FF), F32),
            jax.ShapeDtypeStruct((C, FF), F32),
            jax.ShapeDtypeStruct((9, C, C), F32),
        ),
        in_specs=[pl.BlockSpec(memory_space=VMEM)] * 5,
        out_specs=[pl.BlockSpec(memory_space=VMEM)] * 6,
        compiler_params=pltpu.CompilerParams(vmem_limit_bytes=32 * 2**20),
        name="results",
    )(d_shifted, *halo, sums)


def local(features, cotangent, w_qkv, w_proj, w_fc1, w_fc2, w_conv, gain_attn, gain_mlp, pos_table):
    d_shifted, sums, *halo = call_layer(
        features,
        cotangent,
        w_qkv,
        w_proj,
        w_fc1,
        w_fc2.T,
        w_conv,
        gain_attn.reshape(1, C),
        gain_mlp.reshape(1, C),
        pos_table.T,
    )
    d_features, qkv, proj, fc1, fc2, conv = call_results(d_shifted, halo, sums)
    return d_features, qkv, proj, fc1, fc2.T, conv


def solution(mesh):
    return jax.shard_map(
        local,
        mesh=mesh,
        in_specs=(P("row", "col", None), P("row", "col", None)) + (P(),) * 8,
        out_specs=(P("row", "col", None),) + (P(),) * 5,
        check_vma=False,
    )
```

time: 114 us -> 93.9 us (0.82)
  Pallas kernels: 102 us -> 87.9 us
  local copies, waits for them, and re-layouts: 10.5 us -> 5.08 us
    pallas_call x3 -> x1, Pallas kernels: 99.7 us -> 85.5 us  [call_layer(): pl.pallas_call(layer, out_shape=(jax.ShapeDtypeStruct((NBLK, TOK, C), BF)...]
    unnamed x24 -> x10, local copies, waits for them, and re-layouts: 7.5 us -> 5.08 us
    reshape x2 -> x0, local copies, waits for them, and re-layouts: 1.89 us -> none  [the longest x1 1.12 us: bias_rows(): jnp.broadcast_to(rows, (HEADS, WIN, 15, 2, WIN))]
where the time goes in v1:
time: 93.9 us; the launch traced here: 93.6 us
  Pallas kernels  87.9 us (94%)
  local copies, waits for them, and re-layouts  5.08 us (5%)
    pallas_call x1, Pallas kernels, call_layer(): pl.pallas_call(layer, out_shape=(jax.ShapeDtypeStruct((NBLK, TOK, C), BF)...  85.5 us
    unnamed x10, local copies, waits for them, and re-layouts  5.08 us
    pallas_call x1, Pallas kernels, call_results(): pl.pallas_call(results, out_shape=(jax.ShapeDtypeStruct((ROWS, COLS, C),...  2.39 us

profile of v1, /device:TPU:1, one launch (start us, length us, event | category | flops | bytes accessed | tf_op | source)
XLA Modules:
  0.0 93.6 jit_solution(16126784647622475700)
XLA Ops:
  0.6 85.5 %layer.1 = (bf16[4,512,180]{2,1,0:T(8,128)(2,1)}, bf16[5376,128]{1,0:T(8,128)(2,1)}, bf16[4,64,180]{2,1,0:T(8,128)(2,1)}, bf16[256,180]{1,0:T(8,128)(2,1)}, bf16[32,180]{1,0:T(8,128)(2,1)}) custom-call(bf16[32,64,180]{2,1,0:T(8,128)(2,1)} %f_ref.1, bf16[32,64,180]{2,1,0:T(8,128)(2,1)} %g_ref.1, bf16[180,540]{1,0:T(8,128)(2,1)} %wqkv_ref.1, ...), custom_call_target="tpu_custom_call" | custom-call | tf_op jit(solution)/shard_map/layer/pallas_call | solution.py:627
  86.2 0.0 copy-start
  86.2 1.3 %copy-done = bf16[5376,128]{1,0:T(8,128)(2,1)S(1)} copy-done((bf16[5376,128]{1,0:T(8,128)(2,1)S(1)}, bf16[5376,128]{1,0:T(8,128)(2,1)}, u32[]{:S(2)}) %copy-start) | copy-done | bytes 1376280
  87.5 0.0 copy-start.1
  87.5 1.2 %copy-done.1 = bf16[4,512,180]{2,1,0:T(8,128)(2,1)S(1)} copy-done((bf16[4,512,180]{2,1,0:T(8,128)(2,1)S(1)}, bf16[4,512,180]{2,1,0:T(8,128)(2,1)}, u32[]{:S(2)}) %copy-start.1) | copy-done | bytes 737304
  88.7 0.0 copy-start.2
  88.7 0.9 copy-done.2
  89.6 0.0 copy-start.3
  89.6 0.9 copy-done.3
  90.5 0.0 copy-start.4
  90.5 0.7 copy-done.4
  91.2 2.4 %results.1 = (bf16[32,64,180]{2,1,0:T(8,128)(2,1)}, f32[180,540]{1,0:T(8,128)}, f32[180,180]{1,0:T(8,128)}, f32[180,360]{1,0:T(8,128)}, f32[180,360]{1,0:T(8,128)}, /*index=5*/f32[9,180,180]{2,1,0:T(8,128)}) custom-call(bf16[4,512,180]{2,1,0:T(8,128)(2,1)S(1)} %copy-done.1, bf16[4,64,180]{2,1,0:T(8,128)(2,1)S(1)} %copy-done.2, ...), custom_call_target="tpu_custom_call" | custom-call | tf_op jit(solution)/shard_map/results/pallas_call | solution.py:686
Async XLA Ops:
  86.2 1.3 %copy-start = (bf16[5376,128]{1,0:T(8,128)(2,1)S(1)}, bf16[5376,128]{1,0:T(8,128)(2,1)}, u32[]{:S(2)}) copy-start(bf16[5376,128]{1,0:T(8,128)(2,1)} %get-tuple-element.21.sum_ref) | copy-start | bytes 4128772
  87.5 1.2 %copy-start.1 = (bf16[4,512,180]{2,1,0:T(8,128)(2,1)S(1)}, bf16[4,512,180]{2,1,0:T(8,128)(2,1)}, u32[]{:S(2)}) copy-start(bf16[4,512,180]{2,1,0:T(8,128)(2,1)} %get-tuple-element.17.d_ref) | copy-start | bytes 2211844
  88.7 0.9 copy-start.2
  89.6 0.9 copy-start.3
  90.5 0.7 copy-start.4

commit v2 on v1

--- a/solution.py
+++ b/solution.py
@@ -22,7 +22,7 @@
 TOK = ROWS * BLK
 PAIR = WIN * BLK
 SIDE = 4
-TILES = (22, 6)
+TILES = (14, 12)
 BASE = (0, TILES[0] * CP)
 GROWS = sum(TILES) * CP
 HALVES = tuple(t * CP // 2 for t in TILES)
@@ -122,15 +122,17 @@
 
 
 def layer(
+    f_hbm, g_hbm, wqkv_hbm, wproj_hbm, w1_hbm, w2_hbm, wconv_hbm, g1_hbm, g2_hbm, pos_hbm,
+    d_hbm, sum_hbm, hr_ref, hs_ref, hc_ref,
     f_ref, g_ref, wqkv_ref, wproj_ref, w1_ref, w2_ref, wconv_ref, g1_ref, g2_ref, pos_ref,
-    d_ref, sum_ref, hr_ref, hs_ref, hc_ref,
-    fr_ref, gr_ref, strip_ref, corner_ref, strip_in, strip_out,
+    d_ref, sum_ref,
+    fr_ref, gr_ref, fstrip_ref, gstrip_ref, fcorner_ref, gcorner_ref,
+    fstrip_in, gstrip_in, strip_out,
     grads_ref, core_in0, core_in1, held0, held1, first0, first1, second0, second1, third0, third1,
-    xs, gs, wqkvt, wqkvp, wprojt, wprojp, w1t, w1p, w2t, w2p, wcp, bias,
-    s_x, s_inv1, s_n1, packed, attended, probs, s_norm2, s_inv2, s_n2, s_slope, s_hidden, s_z,
-    dheads, dpacked, s_dmid,
-    a_conv, a_proj, a_fc1, a_fc2, a_qkv,
-    in_send, in_recv, out_send, out_recv, core_send, core_recv, send, recv,
+    xs, gs, wqkvt, wqkvp, wprojt, wprojp, w1t, w1p, w2t, w2p, bias,
+    s_norm1, s_inv1, s_n1, packed, attended, probs, s_norm2, s_inv2, s_n2, s_slope, s_hidden, s_z,
+    dshift, s_dpre, s_dattn, dheads, dpacked, s_dmid,
+    load, store, in_send, in_recv, out_send, out_recv, core_send, core_recv, send, recv,
 ):
     row, col = lax.axis_index("row"), lax.axis_index("col")
     n_row, n_col = lax.axis_size("row"), lax.axis_size("col")
@@ -157,6 +159,11 @@
     for peer in greeted:
         pl.semaphore_signal(barrier, inc=1, device_id=peer, device_id_type=MESH)
 
+    hbm = (f_hbm, g_hbm, wqkv_hbm, wproj_hbm, w1_hbm, w2_hbm, wconv_hbm, g1_hbm, g2_hbm, pos_hbm)
+    own = (f_ref, g_ref, wqkv_ref, wproj_ref, w1_ref, w2_ref, wconv_ref, g1_ref, g2_ref, pos_ref)
+    loads = [pltpu.make_async_copy(s, t, load.at[i]) for i, (s, t) in enumerate(zip(hbm, own))]
+    for c in loads:
+        c.start()
     started = []
 
     def copy(src, dst, s, r, peer):
@@ -167,19 +174,64 @@
         started.append(c)
         return c
 
-    fs = f_ref[:, 0:16, :].astype(F32)[:, 0:8, :]
+    loads[0].wait()
+    fs = f_ref[:, 0:16, :].astype(F32)[:, 0:8, :].reshape(ROWS // 2, 2, 8, C)
+    pairs = jnp.where(iota((ROWS // 2, 8, C), 1) < 4, fs[:, 0], pltpu.roll(fs[:, 1], 4, 1))
+    fstrip_in[...] = low(pairs.reshape(ROWS * 4, C))
+    pl.semaphore_wait(barrier, len(greeted))
+    f_arriving = [
+        copy(fstrip_in.at[0:16], fcorner_ref, in_send.at[0], in_recv.at[0], (up, left)),
+        copy(fstrip_in, fstrip_ref, in_send.at[1], in_recv.at[1], (row, left)),
+        copy(f_ref.at[0:4], fr_ref, in_send.at[2], in_recv.at[2], (up, col)),
+    ]
+    loads[1].wait()
     cs = g_ref[:, 0:16, :].astype(F32)[:, 0:8, :]
-    both = jnp.where(iota((ROWS, 8, C), 1) < 4, fs, pltpu.roll(cs, 4, 1))
-    strip_in[32:288, :] = low(both.reshape(ROWS * 8, C))
-    strip_in[0:32, :] = low(cs[:, 4, :])
-    pl.semaphore_wait(barrier, len(greeted))
-    arriving = [
-        copy(strip_in.at[0:80], corner_ref, in_send.at[3], in_recv.at[3], (up, left)),
-        copy(strip_in, strip_ref, in_send.at[2], in_recv.at[2], (row, left)),
-        copy(f_ref.at[0:4], fr_ref, in_send.at[0], in_recv.at[0], (up, col)),
-        copy(g_ref.at[0:5], gr_ref, in_send.at[1], in_recv.at[1], (up, col)),
+    gstrip_in[...] = low(cs.reshape(ROWS * 8, C))
+    g_arriving = [
+        copy(gstrip_in.at[0:48], gcorner_ref, in_send.at[3], in_recv.at[3], (up, left)),
+        copy(gstrip_in, gstrip_ref, in_send.at[4], in_recv.at[4], (row, left)),
+        copy(g_ref.at[0:5], gr_ref, in_send.at[5], in_recv.at[5], (up, col)),
     ]
 
+    sub = iota((8, C), 0)
+    keep0 = jnp.where((sub == 3) & last_col, 0.0, 1.0)
+    keep2 = jnp.where((sub == 4) & last_col, 0.0, 1.0)
+    LASTB = NBLK - 1
+
+    def put(target, i, rolled):
+        whole = low(rolled[: LASTB * BLK])
+        for b in range(LASTB):
+            target[b, i * BLK : (i + 1) * BLK, :] = whole[b * BLK : (b + 1) * BLK]
+
+    def put_last(target, i, body, last):
+        target[LASTB, i * BLK : (i + 1) * BLK, :] = low(jnp.concatenate([body, last], axis=0))
+
+    def put_x(i, v):
+        put(xs, i, pltpu.roll(v, 60, 0))
+
+    def put_x_last(i, v, extra):
+        r = pltpu.roll(v, 12, 0)
+        put_last(xs, i, r[:8], jnp.where(sub < 4, r[8:], extra))
+
+    def put_g(i, v):
+        for k, turn in enumerate((59, 60, 61)):
+            put(gs.at[k], i, pltpu.roll(v, turn, 0))
+
+    def put_g_last(i, v, extra):
+        for k, n in enumerate((5, 4, 3)):
+            r = pltpu.roll(v, 16 - n, 0)
+            last = jnp.where(sub < 8 - n, r[8:], pltpu.roll(extra, 8 - n, 0))
+            if k != 1:
+                last = last * (keep0, keep2)[k // 2]
+            put_last(gs.at[k], i, r[:8], last)
+
+    for i in range(ROWS - 4):
+        put_x(i, f_ref[i + 4].astype(F32))
+    for i in range(ROWS - 3):
+        put_g(i, g_ref[i + 3].astype(F32))
+
+    for c in loads[2:]:
+        c.wait()
     pad = eye(CP, C)
     sel, sel_one = spread(3 * CP, 3 * C, 0), spread(CP, C, 0)
     wq = low(nn(pad, wqkv_ref[...]))
@@ -192,8 +244,6 @@
     w1t[...] = low(nt(eye(FF, FF), w1p[...]))
     w2t[...] = low(nn(pad, w2_ref[...]))
     w2p[...] = low(nt(eye(FF, FF), w2t[...]))
-    for t in range(9):
-        wcp[t] = low(nn(pad, wconv_ref[t]))
     gain1, gain2 = column(g1_ref), column(g2_ref)
 
     table = pos_ref[...]
@@ -210,52 +260,22 @@
                 start = (WIN - 1 - kr) * BLK
                 at = kr * WIN + kc
                 bias[h, at : at + 1, :] = line[h : h + 1, start : start + PAIR]
-    for acc in (a_conv, a_proj, a_fc1, a_fc2, a_qkv):
-        acc[...] = jnp.zeros_like(acc)
-
-    for c in arriving:
+    dshift[...] = jnp.zeros_like(dshift)
+
+    for c in f_arriving:
         c.wait_recv()
-
-    sub = iota((8, C), 0)
-
-    def tail(body, last):
-        return jnp.concatenate([body[:56], last], axis=0)
-
-    def put_x(i, v, extra):
-        rolled = pltpu.roll(v, 60, 0)
-        whole = low(tail(rolled, jnp.where(sub < 4, rolled[56:], pltpu.roll(extra, 4, 0))))
-        for b in range(NBLK):
-            xs[b, i * BLK : (i + 1) * BLK, :] = whole[b * BLK : (b + 1) * BLK]
-
-    keep0 = jnp.where((sub == 3) & last_col, 0.0, 1.0)
-    keep2 = jnp.where((sub == 4) & last_col, 0.0, 1.0)
-
-    def put_g(i, v, extra, fifth):
-        r5, r4, r3 = pltpu.roll(v, 59, 0), pltpu.roll(v, 60, 0), pltpu.roll(v, 61, 0)
-        e5 = jnp.where(sub == 7, fifth, pltpu.roll(extra, 7, 0))
-        l5 = jnp.where(sub < 3, r5[56:], e5) * keep0
-        l4 = jnp.where(sub < 4, r4[56:], extra)
-        l3 = jnp.where(sub < 5, r3[56:], pltpu.roll(extra, 1, 0)) * keep2
-        for k, (r, last) in enumerate(((r5, l5), (r4, l4), (r3, l3))):
-            whole = low(tail(r, last))
-            for b in range(NBLK):
-                gs[k, b, i * BLK : (i + 1) * BLK, :] = whole[b * BLK : (b + 1) * BLK]
-
-    extras = strip_ref[32:288, :].astype(F32).reshape(ROWS, 8, C)
-    fifths = strip_ref[0:32, :].astype(F32)
-    c_extras = corner_ref[32:80, :].astype(F32).reshape(6, 8, C)
-    c_fifths = corner_ref[0:16, :].astype(F32)
+    quads = fstrip_ref[...].astype(F32).reshape(ROWS // 2, 8, C)
+    corner = fcorner_ref[...].astype(F32).reshape(2, 8, C)
+
+    def quad(source, i):
+        return pltpu.roll(source[i // 2], 4, 0) if i % 2 == 0 else source[i // 2]
+
     for i in range(ROWS):
         if i < ROWS - 4:
-            put_x(i, f_ref[i + 4].astype(F32), extras[i + 4])
+            put_x_last(i, f_ref[i + 4, COLS - 16 :, :].astype(F32), quad(quads, i + 4))
         else:
-            put_x(i, fr_ref[i - 28].astype(F32), c_extras[i - 28])
-    for i in range(ROWS + 2):
-        if i < ROWS - 3:
-            put_g(i, g_ref[i + 3].astype(F32), extras[i + 3], fifths[i + 3 : i + 4])
-        else:
-            k = i - 29
-            put_g(i, gr_ref[k].astype(F32), c_extras[k], c_fifths[k : k + 1])
+            put_x(i, fr_ref[i - 28].astype(F32))
+            put_x_last(i, fr_ref[i - 28, COLS - 16 :, :].astype(F32), quad(corner, i - 28))
 
     lane = iota((1, PAIR), 1)
     second = ((lane >> 3) & 1) == 1
@@ -270,35 +290,37 @@
         x = nt(pad, xs[b])
         centred, inv1 = moments(x)
         normed1 = centred * inv1
-        s_x[b] = normed1
+        s_norm1[b] = normed1
         s_inv1[b] = inv1
         n1 = low(normed1 * gain1)
         s_n1[b] = n1
         packed[b] = low(nn(wqkvt[...], n1))
         col_flag = last_col & (b == NBLK - 1)
 
-        def attend(a, carry):
-            lanes = pl.ds(pl.multiple_of(a * PAIR, PAIR), PAIR)
+        units = [(a, j) for a in range(ROWS // WIN) for j in range(HEADS // 2)]
+        scores = {}
+        for a, j in units:
+            lanes = slice(a * PAIR, (a + 1) * PAIR)
+            q = packed[b, 64 * j : 64 * j + 64, lanes]
+            k = packed[b, CP + 64 * j : CP + 64 * j + 64, lanes]
+            scores[a, j] = tn(k, two_heads(q))
+        soft = {}
+        for a, j in units:
             row_flag = last_row & (a == ROWS // WIN - 1)
             mask = jnp.where((rows_differ & row_flag) | (cols_differ & col_flag), -100.0, 0.0)
-            for j in range(HEADS // 2):
-                q = packed[b, 64 * j : 64 * j + 64, lanes]
-                k = packed[b, CP + 64 * j : CP + 64 * j + 64, lanes]
-                v = packed[b, 2 * CP + 64 * j : 2 * CP + 64 * j + 64, lanes]
-                scores = tn(k, two_heads(q))
-                wide = []
-                for s in range(2):
-                    sc = fold(scores[:, s * PAIR : (s + 1) * PAIR], second)
-                    sc = sc * factor + bias[2 * j + s] + mask
-                    e = jnp.exp(sc - jnp.max(sc, axis=0, keepdims=True))
-                    p = e * (1.0 / jnp.sum(e, axis=0, keepdims=True))
-                    probs[b, a, 2 * j + s] = p
-                    wide.append(unfold(p, second))
-                o = nn(v, jnp.concatenate(wide, axis=1))
-                attended[b, 64 * j : 64 * j + 64, lanes] = low(own_heads(o))
-            return carry
-
-        lax.fori_loop(0, ROWS // WIN, attend, 0, unroll=True)
+            wide = []
+            for s in range(2):
+                sc = fold(scores[a, j][:, s * PAIR : (s + 1) * PAIR], second)
+                sc = sc * factor + bias[2 * j + s] + mask
+                e = jnp.exp(sc - jnp.max(sc, axis=0, keepdims=True))
+                p = e * (1.0 / jnp.sum(e, axis=0, keepdims=True))
+                probs[b, a, 2 * j + s] = p
+                wide.append(unfold(p, second))
+            soft[a, j] = jnp.concatenate(wide, axis=1)
+        for a, j in units:
+            lanes = slice(a * PAIR, (a + 1) * PAIR)
+            v = packed[b, 2 * CP + 64 * j : 2 * CP + 64 * j + 64, lanes]
+            attended[b, 64 * j : 64 * j + 64, lanes] = low(own_heads(nn(v, soft[a, j])))
 
         middle = x + nn(wprojt[...], attended[b])
         centred2, inv2 = moments(middle)
@@ -312,43 +334,52 @@
         hidden = low(pre * cdf)
         s_hidden[b] = hidden
         s_slope[b] = cdf + pre * pdf
-        s_z[b] = low(middle + nn(w2t[...], hidden))
+        z = middle + nn(w2t[...], hidden)
+        s_z[1, b] = low(z)
+        s_z[0, b] = low(jnp.where(drop0, 0.0, z))
+        s_z[2, b] = low(jnp.where(drop2, 0.0, z))
         return carry
 
     lax.fori_loop(0, NBLK, forward, 0)
 
-    def back_to_heads(b, carry):
-        z = s_z[b]
-        z0 = jnp.where(drop0, 0.0, z.astype(F32)).astype(BF)
-        z2 = jnp.where(drop2, 0.0, z.astype(F32)).astype(BF)
-        total = jnp.zeros((CP, TOK), F32)
-        for dy in range(3):
-            part = jnp.zeros((CP, TOK), F32)
-            zd = (z0, z, z2)[dy]
-            for dx in range(3):
-                source = gs[dx, b, (2 - dy) * BLK : (2 - dy) * BLK + TOK, :]
-                part = part + nt(wcp[3 * dy + dx], source)
-                a_conv[3 * dy + dx] += nn(zd, source)
-            if dy == 0:
-                part = jnp.where(drop0, 0.0, part)
-            if dy == 2:
-                part = jnp.where(drop2, 0.0, part)
-            total = total + part
-        d_shift = low(total)
-        a_fc2[:, :FF] += nt(d_shift, s_hidden[b])
-        d_pre = low(nn(w2p[...], d_shift) * s_slope[b])
-        a_fc1[:, :FF] += nt(s_n2[b], d_pre)
-        d_middle = d_shift.astype(F32) + norm_back(
-            nn(w1p[...], d_pre), s_norm2[b], s_inv2[b], gain2
-        )
-        s_dmid[b] = d_middle
-        d_attn = low(d_middle)
-        a_proj[...] += nt(attended[b], d_attn)
-        dheads[b] = low(nn(wprojp[...], d_attn))
-        return carry
-
-    lax.fori_loop(0, NBLK, back_to_heads, 0)
-
+    for c in g_arriving:
+        c.wait_recv()
+    for i in range(ROWS + 2):
+        if i < ROWS - 3:
+            extra = gstrip_ref[(i + 3) * 8 : (i + 4) * 8, :]
+            put_g_last(i, g_ref[i + 3, COLS - 16 :, :].astype(F32), extra.astype(F32))
+        else:
+            k = i - ROWS + 3
+            put_g(i, gr_ref[k].astype(F32))
+            extra = gcorner_ref[k * 8 : (k + 1) * 8, :]
+            put_g_last(i, gr_ref[k, COLS - 16 :, :].astype(F32), extra.astype(F32))
+
+    def tap(b, dy, dx):
+        return gs[dx, b, (2 - dy) * BLK : (2 - dy) * BLK + TOK, :]
+
+    def over_blocks(term):
+        total = term(0)
+        for b in range(1, NBLK):
+            total = total + term(b)
+        return total
+
+    def put_tile(place, tile):
+        grads_ref[place * CP : (place + 1) * CP, :] = low(tile)
+
+    def put_pair(place, left, right):
+        put_tile(place, jnp.concatenate([left, right], axis=1))
+
+    held_back = None
+    for t in range(9):
+        total = over_blocks(lambda b: nn(s_z[t // 3, b], tap(b, t // 3, t % 3)))
+        put_tile(t, total[:, :128])
+        narrow = jnp.concatenate([total[:, 128:], jnp.zeros((CP, 256 - 12 - C), F32)], axis=1)
+        narrow = narrow[:, :64]
+        if t % 2 == 0:
+            held_back = narrow
+        else:
+            put_pair(9 + t // 2, held_back, narrow)
+    put_pair(13, held_back, jnp.zeros((CP, 64), F32))
     steps = (
         (core_in0, held0, first0, second0, third0),
         (core_in1, held1, first1, second1, third1),
@@ -468,69 +499,91 @@
                 )
             )
 
-    def put(place, tile):
-        grads_ref[place * CP : (place + 1) * CP, :] = low(tile)
-
-    half_zero = jnp.zeros((CP, 64), F32)
-    rests = []
-    for t in range(9):
-        put(t, a_conv[t, :, 0:128])
-        rests.append(jnp.concatenate([a_conv[t, :, 128:C], half_zero[:, : 64 - (C - 128)]], axis=1))
-    put(9, a_proj[:, 0:128])
-    rests.append(a_proj[:, 128:192])
-    for i in range(3):
-        put(10 + i, a_fc2[:, i * 128 : (i + 1) * 128])
-        put(13 + i, a_fc1[:, i * 128 : (i + 1) * 128])
-    for i in range(5):
-        put(16 + i, jnp.concatenate([rests[2 * i], rests[2 * i + 1]], axis=1))
-    put(21, jnp.zeros((CP, 128), F32))
     go_core(0)
 
+    def conv_back(b, carry):
+        total = None
+        for dy in range(3):
+            part = None
+            for dx in range(3):
+                product = nt(wconv_ref[3 * dy + dx], tap(b, dy, dx))
+                part = product if part is None else part + product
+            if dy != 1:
+                part = jnp.where((drop0, drop2)[dy // 2], 0.0, part)
+            total = part if total is None else total + part
+        dshift[b, :C, :] = low(total)
+        return carry
+
+    def back_to_heads(b, carry):
+        d_shift = dshift[b]
+        d_pre = low(nn(w2p[...], d_shift) * s_slope[b])
+        s_dpre[b] = d_pre
+        d_middle = d_shift.astype(F32) + norm_back(
+            nn(w1p[...], d_pre), s_norm2[b], s_inv2[b], gain2
+        )
+        s_dmid[b] = d_middle
+        d_attn = low(d_middle)
+        s_dattn[b] = d_attn
+        dheads[b] = low(nn(wprojp[...], d_attn))
+        return carry
+
+    lax.fori_loop(0, NBLK, conv_back, 0)
+    go_first(0)
+    lax.fori_loop(0, NBLK, back_to_heads, 0)
+
+    fc2 = over_blocks(lambda b: nt(dshift[b], s_hidden[b]))
+    fc1 = over_blocks(lambda b: nt(s_n2[b], s_dpre[b]))
+    for place, total in ((14, fc2), (17, fc1)):
+        put_tile(place, total[:, :128])
+        put_tile(place + 1, total[:, 128:256])
+        put_pair(place + 2, total[:, 256:], jnp.zeros((CP, 384 - FF), F32))
+    proj = over_blocks(lambda b: nt(attended[b], s_dattn[b]))
+    put_tile(20, proj[:, :128])
+
     def heads_back(b):
-        def attend_back(a, carry):
-            lanes = pl.ds(pl.multiple_of(a * PAIR, PAIR), PAIR)
-            for j in range(HEADS // 2):
-                q = packed[b, 64 * j : 64 * j + 64, lanes]
-                k = packed[b, CP + 64 * j : CP + 64 * j + 64, lanes]
-                v = packed[b, 2 * CP + 64 * j : 2 * CP + 64 * j + 64, lanes]
-                do = dheads[b, 64 * j : 64 * j + 64, lanes]
-                d_prob = tn(v, two_heads(do))
-                p_wide, s_wide = [], []
-                for s in range(2):
-                    p = probs[b, a, 2 * j + s]
-                    dp = fold(d_prob[:, s * PAIR : (s + 1) * PAIR], second)
-                    ds = p * (dp - jnp.sum(p * dp, axis=0, keepdims=True)) * factor
-                    p_wide.append(unfold(p, second))
-                    s_wide.append(unfold(ds, second))
-                dv = nt(do, jnp.concatenate(p_wide, axis=0))
-                dq = nn(k, jnp.concatenate(s_wide, axis=1))
-                dk = nt(q, jnp.concatenate(s_wide, axis=0))
-                dpacked[b, 64 * j : 64 * j + 64, lanes] = low(own_heads(dq))
-                dpacked[b, CP + 64 * j : CP + 64 * j + 64, lanes] = low(own_heads(dk))
-                dpacked[b, 2 * CP + 64 * j : 2 * CP + 64 * j + 64, lanes] = low(own_heads(dv))
-            return carry
-
-        lax.fori_loop(0, ROWS // WIN, attend_back, 0, unroll=True)
-        a_qkv[...] += nt(s_n1[b], dpacked[b])
+        units = [(a, j) for a in range(ROWS // WIN) for j in range(HEADS // 2)]
+
+        def part(ref, third, a, j):
+            top = third * CP + 64 * j
+            return ref[b, top : top + 64, a * PAIR : (a + 1) * PAIR]
+
+        d_probs = {}
+        for a, j in units:
+            d_probs[a, j] = tn(part(packed, 2, a, j), two_heads(part(dheads, 0, a, j)))
+        p_all, s_all = {}, {}
+        for a, j in units:
+            p_wide, s_wide = [], []
+            for s in range(2):
+                p = probs[b, a, 2 * j + s]
+                dp = fold(d_probs[a, j][:, s * PAIR : (s + 1) * PAIR], second)
+                ds = p * (dp - jnp.sum(p * dp, axis=0, keepdims=True)) * factor
+                p_wide.append(unfold(p, second))
+                s_wide.append(unfold(ds, second))
+            p_all[a, j], s_all[a, j] = p_wide, s_wide
+        for a, j in units:
+            lanes = slice(a * PAIR, (a + 1) * PAIR)
+            dv = nt(part(dheads, 0, a, j), jnp.concatenate(p_all[a, j], axis=0))
+            dq = nn(part(packed, 1, a, j), jnp.concatenate(s_all[a, j], axis=1))
+            dk = nt(part(packed, 0, a, j), jnp.concatenate(s_all[a, j], axis=0))
+            dpacked[b, 64 * j : 64 * j + 64, lanes] = low(own_heads(dq))
+            dpacked[b, CP + 64 * j : CP + 64 * j + 64, lanes] = low(own_heads(dk))
+            dpacked[b, 2 * CP + 64 * j : 2 * CP + 64 * j + 64, lanes] = low(own_heads(dv))
 
     heads_back(0)
-    go_first(0)
     heads_back(1)
     go_second(0)
     heads_back(2)
-    go_third(0)
     heads_back(3)
+    qkv = over_blocks(lambda b: nt(s_n1[b], dpacked[b]))
     for i in range(4):
-        put(22 + i, a_qkv[:, i * 128 : (i + 1) * 128])
-    put(26, jnp.concatenate([a_qkv[:, 512:576], half_zero], axis=1))
-    put(27, jnp.zeros((CP, 128), F32))
+        put_tile(21 + i, qkv[:, i * 128 : (i + 1) * 128])
+    put_pair(25, proj[:, 128:192], qkv[:, 512:576])
     go_core(1)
-    go_back(0)
 
     ones_pair = eye(PAIR, PAIR)
 
     def inputs_back(b):
-        d_in = s_dmid[b] + norm_back(nn(wqkvp[...], dpacked[b]), s_x[b], s_inv1[b], gain1)
+        d_in = s_dmid[b] + norm_back(nn(wqkvp[...], dpacked[b]), s_norm1[b], s_inv1[b], gain1)
         d_low = low(d_in)
         for a in range(ROWS // WIN):
             natural = nt(ones_pair, d_low[:, a * PAIR : (a + 1) * PAIR])
@@ -546,19 +599,35 @@
     ]
     inputs_back(0)
     inputs_back(1)
-    go_second(1)
     inputs_back(2)
     leaving.append(
         copy(d_ref.at[:, 448:512, :], hr_ref, out_send.at[0], out_recv.at[0], (down, col))
     )
+    stores = [pltpu.make_async_copy(d_ref, d_hbm, store.at[0])]
+    stores[0].start()
+    go_third(0)
+    go_second(1)
+    go_back(0)
+    go_third(1)
     go_end(0)
-    go_third(1)
     go_back(1)
+
+    def keep(g):
+        for c in flying[g]["end"]:
+            c.wait_recv()
+        at = slice(BASE[g], BASE[g] + TILES[g] * CP)
+        stores.append(pltpu.make_async_copy(sum_ref.at[at], sum_hbm.at[at], store.at[1 + g]))
+        stores[-1].start()
+
+    keep(0)
     go_end(1)
-    for c in flying[0]["end"] + flying[1]["end"] + leaving:
+    keep(1)
+    for c in leaving:
         c.wait_recv()
     for c in started:
         c.wait_send()
+    for c in stores:
+        c.wait()
 
 
 def call_layer(features, cotangent, w_qkv, w_proj, w_fc1, w_fc2_t, w_conv, g1, g2, table):
@@ -574,12 +643,19 @@
         lead, lengths = sizes
         lead = lead if isinstance(lead, tuple) else (lead,)
         reductions += [VMEM((*lead, n, 128), BF) for n in lengths]
-    scratch = [
+    inputs = (features, cotangent, w_qkv, w_proj, w_fc1, w_fc2_t, w_conv, g1, g2, table)
+    scratch = [VMEM(v.shape, v.dtype) for v in inputs]
+    scratch += [
+        VMEM((NBLK, TOK, C), BF),
+        VMEM((GROWS, 128), BF),
         VMEM((4, COLS, C), BF),
         VMEM((5, COLS, C), BF),
-        VMEM((288, C), BF),
-        VMEM((80, C), BF),
-        VMEM((288, C), BF),
+        VMEM((ROWS * 4, C), BF),
+        VMEM((ROWS * 8, C), BF),
+        VMEM((16, C), BF),
+        VMEM((48, C), BF),
+        VMEM((ROWS * 4, C), BF),
+        VMEM((ROWS * 8, C), BF),
         VMEM((256, C), BF),
         VMEM((GROWS, 128), BF),
         *reductions,
@@ -593,7 +669,6 @@
         VMEM((CP, FF), BF),
         VMEM((CP, FF), BF),
         VMEM((FF, CP), BF),
-        VMEM((9, CP, C), BF),
         VMEM((HEADS, WIN * WIN, PAIR), F32),
         VMEM((NBLK, CP, TOK), F32),
         VMEM((NBLK, 1, TOK), F32),
@@ -606,17 +681,17 @@
         VMEM((NBLK, CP, TOK), BF),
         VMEM((NBLK, FF, TOK), F32),
         VMEM((NBLK, FF, TOK), BF),
+        VMEM((3, NBLK, CP, TOK), BF),
+        VMEM((NBLK, CP, TOK), BF),
+        VMEM((NBLK, FF, TOK), BF),
         VMEM((NBLK, CP, TOK), BF),
         VMEM((NBLK, CP, TOK), BF),
         VMEM((NBLK, 3 * CP, TOK), BF),
         VMEM((NBLK, CP, TOK), F32),
-        VMEM((9, CP, C), F32),
-        VMEM((CP, CP), F32),
-        VMEM((CP, 384), F32),
-        VMEM((CP, 384), F32),
-        VMEM((CP, 3 * CP), F32),
-        pltpu.SemaphoreType.DMA((4,)),
-        pltpu.SemaphoreType.DMA((4,)),
+        pltpu.SemaphoreType.DMA((10,)),
+        pltpu.SemaphoreType.DMA((3,)),
+        pltpu.SemaphoreType.DMA((6,)),
+        pltpu.SemaphoreType.DMA((6,)),
         pltpu.SemaphoreType.DMA((3,)),
         pltpu.SemaphoreType.DMA((3,)),
         pltpu.SemaphoreType.DMA((2, 6)),
@@ -633,19 +708,28 @@
             jax.ShapeDtypeStruct((256, C), BF),
             jax.ShapeDtypeStruct((32, C), BF),
         ),
-        in_specs=[pl.BlockSpec(memory_space=VMEM)] * 10,
-        out_specs=[pl.BlockSpec(memory_space=VMEM)] * 5,
+        in_specs=[pl.BlockSpec(memory_space=pl.ANY)] * 10,
+        out_specs=[pl.BlockSpec(memory_space=pl.ANY)] * 2 + [pl.BlockSpec(memory_space=VMEM)] * 3,
         scratch_shapes=scratch,
         compiler_params=pltpu.CompilerParams(
             collective_id=0, has_side_effects=True, vmem_limit_bytes=60 * 2**20
         ),
         name="layer",
-    )(features, cotangent, w_qkv, w_proj, w_fc1, w_fc2_t, w_conv, g1, g2, table)
+    )(*inputs)
 
 
 def results(
-    d_ref, hr_ref, hs_ref, hc_ref, sum_ref, out_ref, qkv_ref, proj_ref, fc1_ref, fc2_ref, conv_ref
+    d_hbm, hr_hbm, hs_hbm, hc_hbm, sum_hbm,
+    out_ref, qkv_ref, proj_ref, fc1_ref, fc2_ref, conv_ref,
+    d_ref, hr_ref, hs_ref, hc_ref, sum_ref, load,
 ):
+    hbm = (sum_hbm, d_hbm, hr_hbm, hs_hbm, hc_hbm)
+    own = (sum_ref, d_ref, hr_ref, hs_ref, hc_ref)
+    loads = [pltpu.make_async_copy(s, t, load.at[i]) for i, (s, t) in enumerate(zip(hbm, own))]
+    for c in loads:
+        c.start()
+    for c in loads:
+        c.wait()
     sub = iota((8, C), 0)
     extras = hs_ref[...].astype(F32).reshape(ROWS, 8, C)
     corners = hc_ref[...].astype(F32).reshape(4, 8, C)
@@ -666,19 +750,19 @@
         return sum_ref[i * CP : (i + 1) * CP, :]
 
     def rest(i):
-        return full(16 + i // 2)[:, 64 * (i % 2) : 64 * (i % 2) + 64]
+        return full(9 + i // 2)[:, 64 * (i % 2) : 64 * (i % 2) + 64]
 
     def square(i, r):
         return jnp.concatenate([full(i), rest(r)], axis=1)
 
     for t in range(9):
         conv_ref[t] = square(t, t).astype(F32)[:C, :C] * scale
-    proj_ref[...] = nn(spread(CP, C, 1), square(9, 9))[:, :C] * scale
-    fc2 = jnp.concatenate([full(10), full(11), full(12)], axis=1).astype(F32)
+    proj_ref[...] = nn(spread(CP, C, 1), jnp.concatenate([full(20), full(25)[:, :64]], axis=1))[:, :C] * scale
+    fc2 = jnp.concatenate([full(14), full(15), full(16)], axis=1).astype(F32)
     fc2_ref[...] = fc2[:C, :FF] * scale
-    fc1 = jnp.concatenate([full(13), full(14), full(15)], axis=1).astype(F32)
+    fc1 = jnp.concatenate([full(17), full(18), full(19)], axis=1).astype(F32)
     fc1_ref[...] = fc1[:C, :FF] * scale
-    qkv = jnp.concatenate([full(22), full(23), full(24), full(25), full(26)[:, :64]], axis=1)
+    qkv = jnp.concatenate([full(21), full(22), full(23), full(24), full(25)[:, 64:]], axis=1)
     qkv_ref[...] = nn(qkv, spread(3 * CP, 3 * C, 0))[:C] * scale
 
 
@@ -693,8 +777,12 @@
             jax.ShapeDtypeStruct((C, FF), F32),
             jax.ShapeDtypeStruct((9, C, C), F32),
         ),
-        in_specs=[pl.BlockSpec(memory_space=VMEM)] * 5,
+        in_specs=[pl.BlockSpec(memory_space=pl.ANY)] * 5,
         out_specs=[pl.BlockSpec(memory_space=VMEM)] * 6,
+        scratch_shapes=[
+            *(VMEM(v.shape, v.dtype) for v in (d_shifted, *halo, sums)),
+            pltpu.SemaphoreType.DMA((5,)),
+        ],
         compiler_params=pltpu.CompilerParams(vmem_limit_bytes=32 * 2**20),
         name="results",
     )(d_shifted, *halo, sums)

time: 93.9 us -> 72.5 us (0.77)
  Pallas kernels: 87.9 us -> 66.4 us
    pallas_call x1, Pallas kernels: 85.5 us -> 63.2 us  [call_layer(): pl.pallas_call(layer, out_shape=(jax.ShapeDtypeStruct((NBLK, TOK, C), BF)...]
where the time goes in v2:
time: 72.5 us; the launch traced here: 72.3 us
  Pallas kernels  66.4 us (92%)
  local copies, waits for them, and re-layouts  5.05 us (7%)
  between operations  0.82 us (1%)
    pallas_call x1, Pallas kernels, call_layer(): pl.pallas_call(layer, out_shape=(jax.ShapeDtypeStruct((NBLK, TOK, C), BF)...  63.2 us
    unnamed x10, local copies, waits for them, and re-layouts  5.05 us
    pallas_call x1, Pallas kernels, call_results(): pl.pallas_call(results, out_shape=(jax.ShapeDtypeStruct((ROWS, COLS, C),...  3.19 us

profile of v2, /device:TPU:1, one launch (start us, length us, event | category | flops | bytes accessed | tf_op | source)
XLA Modules:
  0.0 72.3 jit_solution(11248445246701609034)
XLA Ops:
  0.6 63.2 %layer.1 = (bf16[4,512,180]{2,1,0:T(8,128)(2,1)}, bf16[4992,128]{1,0:T(8,128)(2,1)}, bf16[4,64,180]{2,1,0:T(8,128)(2,1)}, bf16[256,180]{1,0:T(8,128)(2,1)}, bf16[32,180]{1,0:T(8,128)(2,1)}) custom-call(bf16[32,64,180]{2,1,0:T(8,128)(2,1)} %f_hbm.1, bf16[32,64,180]{2,1,0:T(8,128)(2,1)} %g_hbm.1, bf16[180,540]{1,0:T(8,128)(2,1)} %wqkv_hbm.1, ...), custom_call_target="tpu_custom_call" | custom-call | tf_op jit(solution)/shard_map/layer/pallas_call | solution.py:702
  63.8 0.0 copy-start
  63.9 1.3 %copy-done = bf16[4992,128]{1,0:T(8,128)(2,1)S(1)} copy-done((bf16[4992,128]{1,0:T(8,128)(2,1)S(1)}, bf16[4992,128]{1,0:T(8,128)(2,1)}, u32[]{:S(2)}) %copy-start) | copy-done | bytes 1277976
  65.2 0.0 copy-start.1
  65.2 1.2 %copy-done.1 = bf16[4,512,180]{2,1,0:T(8,128)(2,1)S(1)} copy-done((bf16[4,512,180]{2,1,0:T(8,128)(2,1)S(1)}, bf16[4,512,180]{2,1,0:T(8,128)(2,1)}, u32[]{:S(2)}) %copy-start.1) | copy-done | bytes 737304
  66.4 0.0 copy-start.2
  66.4 0.9 %copy-done.2 = bf16[4,64,180]{2,1,0:T(8,128)(2,1)S(1)} copy-done((bf16[4,64,180]{2,1,0:T(8,128)(2,1)S(1)}, bf16[4,64,180]{2,1,0:T(8,128)(2,1)}, u32[]{:S(2)}) %copy-start.2) | copy-done | bytes 92184
  67.3 0.0 copy-start.3
  67.3 0.9 %copy-done.3 = bf16[256,180]{1,0:T(8,128)(2,1)S(1)} copy-done((bf16[256,180]{1,0:T(8,128)(2,1)S(1)}, bf16[256,180]{1,0:T(8,128)(2,1)}, u32[]{:S(2)}) %copy-start.3) | copy-done | bytes 92184
  68.2 0.0 copy-start.4
  68.2 0.7 copy-done.4
  68.9 3.2 %results.1 = (bf16[32,64,180]{2,1,0:T(8,128)(2,1)}, f32[180,540]{1,0:T(8,128)}, f32[180,180]{1,0:T(8,128)}, f32[180,360]{1,0:T(8,128)}, f32[180,360]{1,0:T(8,128)}, /*index=5*/f32[9,180,180]{2,1,0:T(8,128)}) custom-call(bf16[4,512,180]{2,1,0:T(8,128)(2,1)S(1)} %copy-done.1, bf16[4,64,180]{2,1,0:T(8,128)(2,1)S(1)} %copy-done.2, ...), custom_call_target="tpu_custom_call" | custom-call | tf_op jit(solution)/shard_map/results/pallas_call | solution.py:770
Async XLA Ops:
  63.8 1.3 %copy-start = (bf16[4992,128]{1,0:T(8,128)(2,1)S(1)}, bf16[4992,128]{1,0:T(8,128)(2,1)}, u32[]{:S(2)}) copy-start(bf16[4992,128]{1,0:T(8,128)(2,1)} %get-tuple-element.21.sum_hbm) | copy-start | bytes 3833860
  65.2 1.2 %copy-start.1 = (bf16[4,512,180]{2,1,0:T(8,128)(2,1)S(1)}, bf16[4,512,180]{2,1,0:T(8,128)(2,1)}, u32[]{:S(2)}) copy-start(bf16[4,512,180]{2,1,0:T(8,128)(2,1)} %get-tuple-element.17.d_hbm) | copy-start | bytes 2211844
  66.4 0.9 %copy-start.2 = (bf16[4,64,180]{2,1,0:T(8,128)(2,1)S(1)}, bf16[4,64,180]{2,1,0:T(8,128)(2,1)}, u32[]{:S(2)}) copy-start(bf16[4,64,180]{2,1,0:T(8,128)(2,1)} %get-tuple-element.18.hr_hbm) | copy-start | bytes 276484
  67.3 0.9 %copy-start.3 = (bf16[256,180]{1,0:T(8,128)(2,1)S(1)}, bf16[256,180]{1,0:T(8,128)(2,1)}, u32[]{:S(2)}) copy-start(bf16[256,180]{1,0:T(8,128)(2,1)} %get-tuple-element.19.hs_hbm) | copy-start | bytes 276484
  68.2 0.7 copy-start.4

commit v3 on v2

--- a/solution.py
+++ b/solution.py
@@ -22,8 +22,8 @@
 TOK = ROWS * BLK
 PAIR = WIN * BLK
 SIDE = 4
-TILES = (14, 12)
-BASE = (0, TILES[0] * CP)
+TILES = (14, 8, 6)
+BASE = (0, TILES[0] * CP, (TILES[0] + TILES[1]) * CP)
 GROWS = sum(TILES) * CP
 HALVES = tuple(t * CP // 2 for t in TILES)
 PARTS = tuple(h // 3 for h in HALVES)
@@ -128,11 +128,11 @@
     d_ref, sum_ref,
     fr_ref, gr_ref, fstrip_ref, gstrip_ref, fcorner_ref, gcorner_ref,
     fstrip_in, gstrip_in, strip_out,
-    grads_ref, core_in0, core_in1, held0, held1, first0, first1, second0, second1, third0, third1,
+    grads_ref, first0, first1, first2, second0, second1, second2, third0, third1, third2,
     xs, gs, wqkvt, wqkvp, wprojt, wprojp, w1t, w1p, w2t, w2p, bias,
     s_norm1, s_inv1, s_n1, packed, attended, probs, s_norm2, s_inv2, s_n2, s_slope, s_hidden, s_z,
     dshift, s_dpre, s_dattn, dheads, dpacked, s_dmid,
-    load, store, in_send, in_recv, out_send, out_recv, core_send, core_recv, send, recv,
+    load, store, in_send, in_recv, out_send, out_recv, send, recv,
 ):
     row, col = lax.axis_index("row"), lax.axis_index("col")
     n_row, n_col = lax.axis_size("row"), lax.axis_size("col")
@@ -147,15 +147,17 @@
     def device(xyz, c):
         return ((xyz[0] // 2) * 8 + xyz[2] * 2 + c, lax.rem(xyz[0], 2) * SIDE + xyz[1])
 
-    def along(axis, k):
+    def along(axis, k, other):
         there = list(here)
         there[axis] = lax.rem(there[axis] + k, SIDE)
-        return device(there, core)
+        return device(there, 1 - core if other else core)
 
     sibling = device(here, 1 - core)
+    seven = [(k, other) for k in range(SIDE) for other in (0, 1) if k + other > 0]
     barrier = pltpu.get_barrier_semaphore()
     greeted = [sibling, (up, col), (row, left), (up, left), (down, col), (row, right)]
-    greeted += [(down, right)] + [along(axis, k) for axis in range(3) for k in range(1, SIDE)]
+    greeted += [(down, right)]
+    greeted += [along(axis, k, o) for axis in range(3) for k, o in seven if k > 0]
     for peer in greeted:
         pl.semaphore_signal(barrier, inc=1, device_id=peer, device_id_type=MESH)
 
@@ -262,20 +264,24 @@
                 bias[h, at : at + 1, :] = line[h : h + 1, start : start + PAIR]
     dshift[...] = jnp.zeros_like(dshift)
 
-    for c in f_arriving:
-        c.wait_recv()
-    quads = fstrip_ref[...].astype(F32).reshape(ROWS // 2, 8, C)
-    corner = fcorner_ref[...].astype(F32).reshape(2, 8, C)
-
-    def quad(source, i):
-        return pltpu.roll(source[i // 2], 4, 0) if i % 2 == 0 else source[i // 2]
-
-    for i in range(ROWS):
-        if i < ROWS - 4:
-            put_x_last(i, f_ref[i + 4, COLS - 16 :, :].astype(F32), quad(quads, i + 4))
-        else:
-            put_x(i, fr_ref[i - 28].astype(F32))
-            put_x_last(i, fr_ref[i - 28, COLS - 16 :, :].astype(F32), quad(corner, i - 28))
+    f_arriving[2].wait_recv()
+    for i in range(ROWS - 4, ROWS):
+        put_x(i, fr_ref[i - 28].astype(F32))
+
+    def last_block():
+        f_arriving[1].wait_recv()
+        f_arriving[0].wait_recv()
+        quads = fstrip_ref[...].astype(F32).reshape(ROWS // 2, 8, C)
+        corner = fcorner_ref[...].astype(F32).reshape(2, 8, C)
+
+        def quad(source, i):
+            return pltpu.roll(source[i // 2], 4, 0) if i % 2 == 0 else source[i // 2]
+
+        for i in range(ROWS):
+            if i < ROWS - 4:
+                put_x_last(i, f_ref[i + 4, COLS - 16 :, :].astype(F32), quad(quads, i + 4))
+            else:
+                put_x_last(i, fr_ref[i - 28, COLS - 16 :, :].astype(F32), quad(corner, i - 28))
 
     lane = iota((1, PAIR), 1)
     second = ((lane >> 3) & 1) == 1
@@ -286,61 +292,63 @@
     drop0 = (tok == 27) & last_row
     drop2 = (tok == 28) & last_row
 
-    def forward(b, carry):
-        x = nt(pad, xs[b])
-        centred, inv1 = moments(x)
-        normed1 = centred * inv1
-        s_norm1[b] = normed1
-        s_inv1[b] = inv1
-        n1 = low(normed1 * gain1)
-        s_n1[b] = n1
-        packed[b] = low(nn(wqkvt[...], n1))
-        col_flag = last_col & (b == NBLK - 1)
-
-        units = [(a, j) for a in range(ROWS // WIN) for j in range(HEADS // 2)]
-        scores = {}
-        for a, j in units:
-            lanes = slice(a * PAIR, (a + 1) * PAIR)
-            q = packed[b, 64 * j : 64 * j + 64, lanes]
-            k = packed[b, CP + 64 * j : CP + 64 * j + 64, lanes]
-            scores[a, j] = tn(k, two_heads(q))
-        soft = {}
-        for a, j in units:
+    def forward(step, carry):
+        bs = (2 * step, 2 * step + 1)
+        pl.when(step == 1)(last_block)
+        xv = [nt(pad, xs[b]) for b in bs]
+        for b, x in zip(bs, xv):
+            centred, inv1 = moments(x)
+            normed1 = centred * inv1
+            s_norm1[b] = normed1
+            s_inv1[b] = inv1
+            s_n1[b] = low(normed1 * gain1)
+        for b in bs:
+            packed[b] = low(nn(wqkvt[...], s_n1[b]))
+        units = [(b, a, j) for b in bs for a in range(ROWS // WIN) for j in range(HEADS // 2)]
+
+        def part(b, third, a, j):
+            top = third * CP + 64 * j
+            return packed[b, top : top + 64, a * PAIR : (a + 1) * PAIR]
+
+        scores = [tn(part(b, 1, a, j), two_heads(part(b, 0, a, j))) for b, a, j in units]
+        soft = []
+        for (b, a, j), score in zip(units, scores):
             row_flag = last_row & (a == ROWS // WIN - 1)
+            col_flag = last_col & (b == NBLK - 1)
             mask = jnp.where((rows_differ & row_flag) | (cols_differ & col_flag), -100.0, 0.0)
             wide = []
             for s in range(2):
-                sc = fold(scores[a, j][:, s * PAIR : (s + 1) * PAIR], second)
+                sc = fold(score[:, s * PAIR : (s + 1) * PAIR], second)
                 sc = sc * factor + bias[2 * j + s] + mask
                 e = jnp.exp(sc - jnp.max(sc, axis=0, keepdims=True))
                 p = e * (1.0 / jnp.sum(e, axis=0, keepdims=True))
                 probs[b, a, 2 * j + s] = p
                 wide.append(unfold(p, second))
-            soft[a, j] = jnp.concatenate(wide, axis=1)
-        for a, j in units:
-            lanes = slice(a * PAIR, (a + 1) * PAIR)
-            v = packed[b, 2 * CP + 64 * j : 2 * CP + 64 * j + 64, lanes]
-            attended[b, 64 * j : 64 * j + 64, lanes] = low(own_heads(nn(v, soft[a, j])))
-
-        middle = x + nn(wprojt[...], attended[b])
-        centred2, inv2 = moments(middle)
-        normed2 = centred2 * inv2
-        s_norm2[b] = normed2
-        s_inv2[b] = inv2
-        n2 = low(normed2 * gain2)
-        s_n2[b] = n2
-        pre = nn(w1t[...], n2)
-        cdf, pdf = gelu_parts(pre)
-        hidden = low(pre * cdf)
-        s_hidden[b] = hidden
-        s_slope[b] = cdf + pre * pdf
-        z = middle + nn(w2t[...], hidden)
-        s_z[1, b] = low(z)
-        s_z[0, b] = low(jnp.where(drop0, 0.0, z))
-        s_z[2, b] = low(jnp.where(drop2, 0.0, z))
+            soft.append(jnp.concatenate(wide, axis=1))
+        for (b, a, j), wide in zip(units, soft):
+            o = nn(part(b, 2, a, j), wide)
+            attended[b, 64 * j : 64 * j + 64, a * PAIR : (a + 1) * PAIR] = low(own_heads(o))
+
+        middles = [x + nn(wprojt[...], attended[b]) for b, x in zip(bs, xv)]
+        for b, middle in zip(bs, middles):
+            centred2, inv2 = moments(middle)
+            normed2 = centred2 * inv2
+            s_norm2[b] = normed2
+            s_inv2[b] = inv2
+            s_n2[b] = low(normed2 * gain2)
+        pres = [nn(w1t[...], s_n2[b]) for b in bs]
+        for b, pre in zip(bs, pres):
+            cdf, pdf = gelu_parts(pre)
+            s_hidden[b] = low(pre * cdf)
+            s_slope[b] = cdf + pre * pdf
+        for b, middle in zip(bs, middles):
+            z = middle + nn(w2t[...], s_hidden[b])
+            s_z[1, b] = low(z)
+            s_z[0, b] = low(jnp.where(drop0, 0.0, z))
+            s_z[2, b] = low(jnp.where(drop2, 0.0, z))
         return carry
 
-    lax.fori_loop(0, NBLK, forward, 0)
+    lax.fori_loop(0, NBLK // 2, forward, 0)
 
     for c in g_arriving:
         c.wait_recv()
@@ -380,52 +388,35 @@
         else:
             put_pair(9 + t // 2, held_back, narrow)
     put_pair(13, held_back, jnp.zeros((CP, 64), F32))
-    steps = (
-        (core_in0, held0, first0, second0, third0),
-        (core_in1, held1, first1, second1, third1),
-    )
-    flying = [{}, {}]
+    steps = ((first0, second0, third0), (first1, second1, third1), (first2, second2, third2))
+    flying = [{}, {}, {}]
 
     def rows(start, size):
         return pl.ds(pl.multiple_of(start, 16), size)
 
-    def at_part(g, c, p):
-        return BASE[g] + c * HALVES[g] + p * PARTS[g]
-
-    def go_core(g):
-        flying[g]["core"] = [
-            copy(
-                grads_ref.at[rows(at_part(g, 1 - core, p), PARTS[g])],
-                steps[g][0].at[p],
-                core_send.at[g, p],
-                core_recv.at[g, p],
-                sibling,
-            )
+    def share_rows(g, c, p, share):
+        at = BASE[g] + c * HALVES[g] + p * PARTS[g] + share * SHARES[g]
+        return rows(at, SHARES[g])
+
+    def go_first(g):
+        flying[g]["first"] = [
+            [
+                copy(
+                    grads_ref.at[
+                        share_rows(g, 1 - core if o else core, p, lax.rem(here[p] + k, SIDE))
+                    ],
+                    steps[g][0].at[p, i],
+                    send.at[g, 0, p, i],
+                    recv.at[g, 0, p, i],
+                    along(p, k, o),
+                )
+                for i, (k, o) in enumerate(seven)
+            ]
             for p in range(3)
         ]
 
-    def go_first(g):
-        core_in, held, first = steps[g][:3]
-        flying[g]["first"] = []
-        for p in range(3):
-            flying[g]["core"][p].wait_recv()
-            own = grads_ref[rows(at_part(g, core, p), PARTS[g]), :].astype(F32)
-            held[p] = low(own + core_in[p].astype(F32))
-            group = []
-            for k in range(1, SIDE):
-                share = lax.rem(here[p] + k, SIDE)
-                group.append(
-                    copy(
-                        held.at[p, rows(share * SHARES[g], SHARES[g])],
-                        first.at[p, k - 1],
-                        send.at[g, 0, p, k - 1],
-                        recv.at[g, 0, p, k - 1],
-                        along(p, k),
-                    )
-                )
-            flying[g]["first"].append(group)
-
-    def spread_out(g, p, step, source, target, axis):
+    def spread_out(g, p, step, source, axis):
+        target = steps[g][step]
         target[p, here[axis]] = source
         return [
             copy(
@@ -433,7 +424,7 @@
                 target.at[p, here[axis]],
                 send.at[g, step, p, k - 1],
                 recv.at[g, step, p, k - 1],
-                along(axis, k),
+                along(axis, k, 0),
             )
             for k in range(1, SIDE)
         ]
@@ -447,59 +438,37 @@
         return low(total)
 
     def go_second(g):
-        held, first, second_in = steps[g][1:4]
         flying[g]["second"] = []
         for p in range(3):
-            total = held[p, rows(here[p] * SHARES[g], SHARES[g]), :].astype(F32)
-            for k in range(1, SIDE):
-                flying[g]["first"][p][k - 1].wait_recv()
-                total = total + first[p, k - 1].astype(F32)
-            flying[g]["second"].append(
-                spread_out(g, p, 1, low(total), second_in, (p + 1) % 3)
-            )
+            total = grads_ref[share_rows(g, core, p, here[p]), :].astype(F32)
+            for i in range(len(seven)):
+                flying[g]["first"][p][i].wait_recv()
+                total = total + steps[g][0][p, i].astype(F32)
+            flying[g]["second"].append(spread_out(g, p, 1, low(total), (p + 1) % 3))
 
     def go_third(g):
-        second_in, third_in = steps[g][3:5]
         flying[g]["third"] = []
         for p in range(3):
-            total = gathered(flying[g]["second"][p], second_in, p)
-            flying[g]["third"].append(spread_out(g, p, 2, total, third_in, (p + 2) % 3))
+            total = gathered(flying[g]["second"][p], steps[g][1], p)
+            flying[g]["third"].append(spread_out(g, p, 2, total, (p + 2) % 3))
 
     def go_back(g):
-        flying[g]["back"] = []
-        for p in range(3):
-            at = rows(at_part(g, core, p) + here[p] * SHARES[g], SHARES[g])
-            sum_ref[at, :] = gathered(flying[g]["third"][p], steps[g][4], p)
-            flying[g]["back"].append(
-                [
-                    copy(
-                        sum_ref.at[at],
-                        sum_ref.at[at],
-                        send.at[g, 3, p, k - 1],
-                        recv.at[g, 3, p, k - 1],
-                        along(p, k),
-                    )
-                    for k in range(1, SIDE)
-                ]
-            )
-
-    def go_end(g):
         flying[g]["end"] = []
         for p in range(3):
-            for c in flying[g]["back"][p]:
-                c.wait_recv()
-            at = rows(at_part(g, core, p), PARTS[g])
-            flying[g]["end"].append(
+            at = share_rows(g, core, p, here[p])
+            sum_ref[at, :] = gathered(flying[g]["third"][p], steps[g][2], p)
+            flying[g]["end"] += [
                 copy(
                     sum_ref.at[at],
                     sum_ref.at[at],
-                    core_send.at[g, 3 + p],
-                    core_recv.at[g, 3 + p],
-                    sibling,
+                    send.at[g, 3, p, i],
+                    recv.at[g, 3, p, i],
+                    along(p, k, o),
                 )
-            )
-
-    go_core(0)
+                for i, (k, o) in enumerate(seven)
+            ]
+
+    go_first(0)
 
     def conv_back(b, carry):
         total = None
@@ -514,22 +483,25 @@
         dshift[b, :C, :] = low(total)
         return carry
 
-    def back_to_heads(b, carry):
-        d_shift = dshift[b]
-        d_pre = low(nn(w2p[...], d_shift) * s_slope[b])
-        s_dpre[b] = d_pre
-        d_middle = d_shift.astype(F32) + norm_back(
-            nn(w1p[...], d_pre), s_norm2[b], s_inv2[b], gain2
-        )
-        s_dmid[b] = d_middle
-        d_attn = low(d_middle)
-        s_dattn[b] = d_attn
-        dheads[b] = low(nn(wprojp[...], d_attn))
+    def back_to_heads(step, carry):
+        bs = (2 * step, 2 * step + 1)
+        d_pres = [low(nn(w2p[...], dshift[b]) * s_slope[b]) for b in bs]
+        d_middles = []
+        for b, d_pre in zip(bs, d_pres):
+            s_dpre[b] = d_pre
+            d_middle = dshift[b].astype(F32) + norm_back(
+                nn(w1p[...], d_pre), s_norm2[b], s_inv2[b], gain2
+            )
+            s_dmid[b] = d_middle
+            d_middles.append(low(d_middle))
+        for b, d_attn in zip(bs, d_middles):
+            s_dattn[b] = d_attn
+            dheads[b] = low(nn(wprojp[...], d_attn))
         return carry
 
     lax.fori_loop(0, NBLK, conv_back, 0)
-    go_first(0)
-    lax.fori_loop(0, NBLK, back_to_heads, 0)
+    lax.fori_loop(0, NBLK // 2, back_to_heads, 0)
+    go_second(0)
 
     fc2 = over_blocks(lambda b: nt(dshift[b], s_hidden[b]))
     fc1 = over_blocks(lambda b: nt(s_n2[b], s_dpre[b]))
@@ -539,6 +511,8 @@
         put_pair(place + 2, total[:, 256:], jnp.zeros((CP, 384 - FF), F32))
     proj = over_blocks(lambda b: nt(attended[b], s_dattn[b]))
     put_tile(20, proj[:, :128])
+    put_pair(21, proj[:, 128:192], jnp.zeros((CP, 64), F32))
+    go_first(1)
 
     def heads_back(b):
         units = [(a, j) for a in range(ROWS // WIN) for j in range(HEADS // 2)]
@@ -571,14 +545,16 @@
 
     heads_back(0)
     heads_back(1)
-    go_second(0)
+    go_third(0)
     heads_back(2)
     heads_back(3)
     qkv = over_blocks(lambda b: nt(s_n1[b], dpacked[b]))
     for i in range(4):
-        put_tile(21 + i, qkv[:, i * 128 : (i + 1) * 128])
-    put_pair(25, proj[:, 128:192], qkv[:, 512:576])
-    go_core(1)
+        put_tile(22 + i, qkv[:, i * 128 : (i + 1) * 128])
+    put_pair(26, qkv[:, 512:576], jnp.zeros((CP, 64), F32))
+    put_tile(27, jnp.zeros((CP, 128), F32))
+    go_first(2)
+    go_second(1)
 
     ones_pair = eye(PAIR, PAIR)
 
@@ -590,7 +566,6 @@
             d_ref[b, a * PAIR : (a + 1) * PAIR, :] = low(natural[:, :C])
 
     inputs_back(NBLK - 1)
-    go_first(1)
     edge = d_ref[NBLK - 1].astype(F32).reshape(ROWS, 2, 8, C)[:, 1]
     strip_out[...] = low(edge.reshape(ROWS * 8, C))
     leaving = [
@@ -605,12 +580,6 @@
     )
     stores = [pltpu.make_async_copy(d_ref, d_hbm, store.at[0])]
     stores[0].start()
-    go_third(0)
-    go_second(1)
-    go_back(0)
-    go_third(1)
-    go_end(0)
-    go_back(1)
 
     def keep(g):
         for c in flying[g]["end"]:
@@ -619,9 +588,15 @@
         stores.append(pltpu.make_async_copy(sum_ref.at[at], sum_hbm.at[at], store.at[1 + g]))
         stores[-1].start()
 
+    go_back(0)
+    go_second(2)
+    go_third(1)
+    go_third(2)
+    go_back(1)
     keep(0)
-    go_end(1)
+    go_back(2)
     keep(1)
+    keep(2)
     for c in leaving:
         c.wait_recv()
     for c in started:
@@ -633,16 +608,8 @@
 def call_layer(features, cotangent, w_qkv, w_proj, w_fc1, w_fc2_t, w_conv, g1, g2, table):
     blocks = ROWS // WIN
     reductions = []
-    for sizes in (
-        (3, PARTS),
-        (3, PARTS),
-        ((3, SIDE - 1), SHARES),
-        ((3, SIDE), SHARES),
-        ((3, SIDE), SHARES),
-    ):
-        lead, lengths = sizes
-        lead = lead if isinstance(lead, tuple) else (lead,)
-        reductions += [VMEM((*lead, n, 128), BF) for n in lengths]
+    for slots in (2 * SIDE - 1, SIDE, SIDE):
+        reductions += [VMEM((3, slots, n, 128), BF) for n in SHARES]
     inputs = (features, cotangent, w_qkv, w_proj, w_fc1, w_fc2_t, w_conv, g1, g2, table)
     scratch = [VMEM(v.shape, v.dtype) for v in inputs]
     scratch += [
@@ -689,15 +656,13 @@
         VMEM((NBLK, 3 * CP, TOK), BF),
         VMEM((NBLK, CP, TOK), F32),
         pltpu.SemaphoreType.DMA((10,)),
-        pltpu.SemaphoreType.DMA((3,)),
+        pltpu.SemaphoreType.DMA((4,)),
         pltpu.SemaphoreType.DMA((6,)),
         pltpu.SemaphoreType.DMA((6,)),
         pltpu.SemaphoreType.DMA((3,)),
         pltpu.SemaphoreType.DMA((3,)),
-        pltpu.SemaphoreType.DMA((2, 6)),
-        pltpu.SemaphoreType.DMA((2, 6)),
-        pltpu.SemaphoreType.DMA((2, 4, 3, SIDE - 1)),
-        pltpu.SemaphoreType.DMA((2, 4, 3, SIDE - 1)),
+        pltpu.SemaphoreType.DMA((3, 4, 3, 2 * SIDE - 1)),
+        pltpu.SemaphoreType.DMA((3, 4, 3, 2 * SIDE - 1)),
     ]
     return pl.pallas_call(
         layer,
@@ -720,15 +685,22 @@
 
 def results(
     d_hbm, hr_hbm, hs_hbm, hc_hbm, sum_hbm,
-    out_ref, qkv_ref, proj_ref, fc1_ref, fc2_ref, conv_ref,
-    d_ref, hr_ref, hs_ref, hc_ref, sum_ref, load,
+    out_hbm, qkv_hbm, proj_hbm, fc1_hbm, fc2_hbm, conv_hbm,
+    d_ref, hr_ref, hs_ref, hc_ref, sum_ref,
+    out_ref, qkv_ref, proj_ref, fc1_ref, fc2_ref, conv_ref, load, store,
 ):
-    hbm = (sum_hbm, d_hbm, hr_hbm, hs_hbm, hc_hbm)
-    own = (sum_ref, d_ref, hr_ref, hs_ref, hc_ref)
+    hbm = (hr_hbm, hs_hbm, hc_hbm, d_hbm, sum_hbm)
+    own = (hr_ref, hs_ref, hc_ref, d_ref, sum_ref)
     loads = [pltpu.make_async_copy(s, t, load.at[i]) for i, (s, t) in enumerate(zip(hbm, own))]
     for c in loads:
         c.start()
-    for c in loads:
+    stores = []
+
+    def keep(source, target):
+        stores.append(pltpu.make_async_copy(source, target, store.at[len(stores)]))
+        stores[-1].start()
+
+    for c in loads[:4]:
         c.wait()
     sub = iota((8, C), 0)
     extras = hs_ref[...].astype(F32).reshape(ROWS, 8, C)
@@ -744,6 +716,8 @@
         head = jnp.where(sub < 4, pltpu.roll(extra, 4, 0), v[:8])
         out_ref[i] = low(jnp.concatenate([head, v[8:]], axis=0))
 
+    keep(out_ref, out_hbm)
+    loads[4].wait()
     scale = 1.0 / math.sqrt(ROWS * COLS * lax.axis_size("row") * lax.axis_size("col"))
 
     def full(i):
@@ -757,35 +731,45 @@
 
     for t in range(9):
         conv_ref[t] = square(t, t).astype(F32)[:C, :C] * scale
-    proj_ref[...] = nn(spread(CP, C, 1), jnp.concatenate([full(20), full(25)[:, :64]], axis=1))[:, :C] * scale
+    keep(conv_ref, conv_hbm)
+    proj_ref[...] = nn(spread(CP, C, 1), jnp.concatenate([full(20), full(21)[:, :64]], axis=1))[:, :C] * scale
+    keep(proj_ref, proj_hbm)
     fc2 = jnp.concatenate([full(14), full(15), full(16)], axis=1).astype(F32)
     fc2_ref[...] = fc2[:C, :FF] * scale
+    keep(fc2_ref, fc2_hbm)
     fc1 = jnp.concatenate([full(17), full(18), full(19)], axis=1).astype(F32)
     fc1_ref[...] = fc1[:C, :FF] * scale
-    qkv = jnp.concatenate([full(21), full(22), full(23), full(24), full(25)[:, 64:]], axis=1)
+    keep(fc1_ref, fc1_hbm)
+    qkv = jnp.concatenate([full(22), full(23), full(24), full(25), full(26)[:, :64]], axis=1)
     qkv_ref[...] = nn(qkv, spread(3 * CP, 3 * C, 0))[:C] * scale
+    keep(qkv_ref, qkv_hbm)
+    for c in stores:
+        c.wait()
 
 
 def call_results(d_shifted, halo, sums):
+    operands = (d_shifted, *halo, sums)
+    shapes = (
+        jax.ShapeDtypeStruct((ROWS, COLS, C), BF),
+        jax.ShapeDtypeStruct((C, 3 * C), F32),
+        jax.ShapeDtypeStruct((C, C), F32),
+        jax.ShapeDtypeStruct((C, FF), F32),
+        jax.ShapeDtypeStruct((C, FF), F32),
+        jax.ShapeDtypeStruct((9, C, C), F32),
+    )
     return pl.pallas_call(
         results,
-        out_shape=(
-            jax.ShapeDtypeStruct((ROWS, COLS, C), BF),
-            jax.ShapeDtypeStruct((C, 3 * C), F32),
-            jax.ShapeDtypeStruct((C, C), F32),
-            jax.ShapeDtypeStruct((C, FF), F32),
-            jax.ShapeDtypeStruct((C, FF), F32),
-            jax.ShapeDtypeStruct((9, C, C), F32),
-        ),
+        out_shape=shapes,
         in_specs=[pl.BlockSpec(memory_space=pl.ANY)] * 5,
-        out_specs=[pl.BlockSpec(memory_space=VMEM)] * 6,
+        out_specs=[pl.BlockSpec(memory_space=pl.ANY)] * 6,
         scratch_shapes=[
-            *(VMEM(v.shape, v.dtype) for v in (d_shifted, *halo, sums)),
+            *(VMEM(v.shape, v.dtype) for v in operands + shapes),
             pltpu.SemaphoreType.DMA((5,)),
+            pltpu.SemaphoreType.DMA((6,)),
         ],
-        compiler_params=pltpu.CompilerParams(vmem_limit_bytes=32 * 2**20),
+        compiler_params=pltpu.CompilerParams(vmem_limit_bytes=60 * 2**20),
         name="results",
-    )(d_shifted, *halo, sums)
+    )(*operands)
 
 
 def local(features, cotangent, w_qkv, w_proj, w_fc1, w_fc2, w_conv, gain_attn, gain_mlp, pos_table):

time: 72.5 us -> 66.6 us (0.919)
  local copies, waits for them, and re-layouts: 5.05 us -> 0 us
  Pallas kernels: 66.4 us -> 65.6 us
    unnamed x10 -> x0, local copies, waits for them, and re-layouts: 5.05 us -> none
    pallas_call x1, Pallas kernels: 63.2 us -> 61.6 us  [call_layer(): pl.pallas_call(layer, out_shape=(jax.ShapeDtypeStruct((NBLK, TOK, C), BF)...]
    pallas_call x1, Pallas kernels: 3.19 us -> 4 us  [call_results(): pl.pallas_call(results, out_shape=shapes, in_specs=[pl.BlockSpec(memory_s...]
where the time goes in v3:
time: 66.6 us; the launch traced here: 66.4 us
  Pallas kernels  65.6 us (98%)
  between operations  0.8 us (1%)
    pallas_call x1, Pallas kernels, call_layer(): pl.pallas_call(layer, out_shape=(jax.ShapeDtypeStruct((NBLK, TOK, C), BF)...  61.6 us
    pallas_call x1, Pallas kernels, call_results(): pl.pallas_call(results, out_shape=shapes, in_specs=[pl.BlockSpec(memory_s...  4 us

profile of v3, /device:TPU:1, one launch (start us, length us, event | category | flops | bytes accessed | tf_op | source)
XLA Modules:
  0.0 66.4 jit_solution(17763606101564505762)
XLA Ops:
  0.6 61.6 %layer.1 = (bf16[4,512,180]{2,1,0:T(8,128)(2,1)}, bf16[5376,128]{1,0:T(8,128)(2,1)}, bf16[4,64,180]{2,1,0:T(8,128)(2,1)}, bf16[256,180]{1,0:T(8,128)(2,1)}, bf16[32,180]{1,0:T(8,128)(2,1)}) custom-call(bf16[32,64,180]{2,1,0:T(8,128)(2,1)} %f_hbm.1, bf16[32,64,180]{2,1,0:T(8,128)(2,1)} %g_hbm.1, bf16[180,540]{1,0:T(8,128)(2,1)} %wqkv_hbm.1, ...), custom_call_target="tpu_custom_call" | custom-call | tf_op jit(solution)/shard_map/layer/pallas_call | solution.py:667
  62.3 4.0 %results.1 = (bf16[32,64,180]{2,1,0:T(8,128)(2,1)}, f32[180,540]{1,0:T(8,128)}, f32[180,180]{1,0:T(8,128)}, f32[180,360]{1,0:T(8,128)}, f32[180,360]{1,0:T(8,128)}, /*index=5*/f32[9,180,180]{2,1,0:T(8,128)}) custom-call(bf16[4,512,180]{2,1,0:T(8,128)(2,1)} %get-tuple-element.17.d_hbm, bf16[4,64,180]{2,1,0:T(8,128)(2,1)} %get-tuple-element.18.hr_hbm, ...), custom_call_target="tpu_custom_call" | custom-call | tf_op jit(solution)/shard_map/results/pallas_call | solution.py:760

commit v4 on v3

--- a/solution.py
+++ b/solution.py
@@ -21,6 +21,9 @@
 NBLK = COLS // BLK
 TOK = ROWS * BLK
 PAIR = WIN * BLK
+UT = TOK // 2
+UNITS = 8
+PAIRS = UT // PAIR
 SIDE = 4
 TILES = (14, 8, 6)
 BASE = (0, TILES[0] * CP, (TILES[0] + TILES[1]) * CP)
@@ -128,11 +131,11 @@
     d_ref, sum_ref,
     fr_ref, gr_ref, fstrip_ref, gstrip_ref, fcorner_ref, gcorner_ref,
     fstrip_in, gstrip_in, strip_out,
-    grads_ref, first0, first1, first2, second0, second1, second2, third0, third1, third2,
+    grads_ref, core0, core1, held0, held1, first0, first1, first2, second0, second1, second2, third0, third1, third2,
     xs, gs, wqkvt, wqkvp, wprojt, wprojp, w1t, w1p, w2t, w2p, bias,
     s_norm1, s_inv1, s_n1, packed, attended, probs, s_norm2, s_inv2, s_n2, s_slope, s_hidden, s_z,
     dshift, s_dpre, s_dattn, dheads, dpacked, s_dmid,
-    load, store, in_send, in_recv, out_send, out_recv, send, recv,
+    load, store, in_send, in_recv, out_send, out_recv, core_send, core_recv, send, recv,
 ):
     row, col = lax.axis_index("row"), lax.axis_index("col")
     n_row, n_col = lax.axis_size("row"), lax.axis_size("col")
@@ -264,9 +267,10 @@
                 bias[h, at : at + 1, :] = line[h : h + 1, start : start + PAIR]
     dshift[...] = jnp.zeros_like(dshift)
 
-    f_arriving[2].wait_recv()
-    for i in range(ROWS - 4, ROWS):
-        put_x(i, fr_ref[i - 28].astype(F32))
+    def last_rows():
+        f_arriving[2].wait_recv()
+        for i in range(ROWS - 4, ROWS):
+            put_x(i, fr_ref[i - 28].astype(F32))
 
     def last_block():
         f_arriving[1].wait_recv()
@@ -288,14 +292,21 @@
     k_sub, q_lane = iota((WIN * WIN, PAIR), 0), iota((WIN * WIN, PAIR), 1)
     rows_differ = ((k_sub >> 5) & 1) != ((q_lane >> 6) & 1)
     cols_differ = (((k_sub >> 2) & 1) != ((q_lane >> 2) & 1)) & (((q_lane >> 3) & 1) == 1)
-    tok = iota((1, TOK), 1) >> 4
-    drop0 = (tok == 27) & last_row
-    drop2 = (tok == 28) & last_row
-
-    def forward(step, carry):
-        bs = (2 * step, 2 * step + 1)
-        pl.when(step == 1)(last_block)
-        xv = [nt(pad, xs[b]) for b in bs]
+    tok = iota((1, UT), 1) >> 4
+
+    def place_of(u):
+        t = u // 6
+        return (1 - t) * (u % 3) + 3 * t, (1 - t) * (u // 3) + t * (u - 6)
+
+    def lines(start, size):
+        return pl.ds(start if isinstance(start, int) else pl.multiple_of(start, 16), size)
+
+    def drops(half):
+        return (tok == 27 - 16 * half) & last_row, (tok == 28 - 16 * half) & last_row
+
+    def forward(*bs):
+        at = [place_of(u) for u in bs]
+        xv = [nt(pad, xs[b, lines(half * UT, UT), :]) for b, half in at]
         for b, x in zip(bs, xv):
             centred, inv1 = moments(x)
             normed1 = centred * inv1
@@ -304,7 +315,7 @@
             s_n1[b] = low(normed1 * gain1)
         for b in bs:
             packed[b] = low(nn(wqkvt[...], s_n1[b]))
-        units = [(b, a, j) for b in bs for a in range(ROWS // WIN) for j in range(HEADS // 2)]
+        units = [(b, a, j) for b in bs for a in range(PAIRS) for j in range(HEADS // 2)]
 
         def part(b, third, a, j):
             top = third * CP + 64 * j
@@ -313,8 +324,9 @@
         scores = [tn(part(b, 1, a, j), two_heads(part(b, 0, a, j))) for b, a, j in units]
         soft = []
         for (b, a, j), score in zip(units, scores):
-            row_flag = last_row & (a == ROWS // WIN - 1)
-            col_flag = last_col & (b == NBLK - 1)
+            block, half = place_of(b)
+            row_flag = last_row & (half * PAIRS + a == ROWS // WIN - 1)
+            col_flag = last_col & (block == NBLK - 1)
             mask = jnp.where((rows_differ & row_flag) | (cols_differ & col_flag), -100.0, 0.0)
             wide = []
             for s in range(2):
@@ -341,14 +353,17 @@
             cdf, pdf = gelu_parts(pre)
             s_hidden[b] = low(pre * cdf)
             s_slope[b] = cdf + pre * pdf
-        for b, middle in zip(bs, middles):
+        for b, (_, half), middle in zip(bs, at, middles):
+            drop0, drop2 = drops(half)
             z = middle + nn(w2t[...], s_hidden[b])
             s_z[1, b] = low(z)
             s_z[0, b] = low(jnp.where(drop0, 0.0, z))
             s_z[2, b] = low(jnp.where(drop2, 0.0, z))
-        return carry
-
-    lax.fori_loop(0, NBLK // 2, forward, 0)
+
+    forward(0, 1, 2)
+    last_rows()
+    last_block()
+    forward(3, 4, 5, 6, 7)
 
     for c in g_arriving:
         c.wait_recv()
@@ -365,6 +380,12 @@
     def tap(b, dy, dx):
         return gs[dx, b, (2 - dy) * BLK : (2 - dy) * BLK + TOK, :]
 
+    def halves(b):
+        return (b, b + 3) if b < NBLK - 1 else (6, 7)
+
+    def both(ref, b):
+        return jnp.concatenate([ref[u] for u in halves(b)], axis=1)
+
     def over_blocks(term):
         total = term(0)
         for b in range(1, NBLK):
@@ -379,7 +400,7 @@
 
     held_back = None
     for t in range(9):
-        total = over_blocks(lambda b: nn(s_z[t // 3, b], tap(b, t // 3, t % 3)))
+        total = over_blocks(lambda b: nn(both(s_z.at[t // 3], b), tap(b, t // 3, t % 3)))
         put_tile(t, total[:, :128])
         narrow = jnp.concatenate([total[:, 128:], jnp.zeros((CP, 256 - 12 - C), F32)], axis=1)
         narrow = narrow[:, :64]
@@ -389,6 +410,7 @@
             put_pair(9 + t // 2, held_back, narrow)
     put_pair(13, held_back, jnp.zeros((CP, 64), F32))
     steps = ((first0, second0, third0), (first1, second1, third1), (first2, second2, third2))
+    staged = ((core0, held0), (core1, held1))
     flying = [{}, {}, {}]
 
     def rows(start, size):
@@ -398,7 +420,42 @@
         at = BASE[g] + c * HALVES[g] + p * PARTS[g] + share * SHARES[g]
         return rows(at, SHARES[g])
 
+    def part_rows(g, c, p):
+        return rows(BASE[g] + c * HALVES[g] + p * PARTS[g], PARTS[g])
+
+    def go_core(g):
+        flying[g]["core"] = [
+            copy(
+                grads_ref.at[part_rows(g, 1 - core, p)],
+                staged[g][0].at[p],
+                core_send.at[g, p],
+                core_recv.at[g, p],
+                sibling,
+            )
+            for p in range(3)
+        ]
+
     def go_first(g):
+        if g < 2:
+            flying[g]["first"] = []
+            for p in range(3):
+                flying[g]["core"][p].wait_recv()
+                total = grads_ref[part_rows(g, core, p), :].astype(F32)
+                staged[g][1][p] = low(total + staged[g][0][p].astype(F32))
+                group = []
+                for k in range(1, SIDE):
+                    share = lax.rem(here[p] + k, SIDE)
+                    group.append(
+                        copy(
+                            staged[g][1].at[p, rows(share * SHARES[g], SHARES[g])],
+                            steps[g][0].at[p, k - 1],
+                            send.at[g, 0, p, k - 1],
+                            recv.at[g, 0, p, k - 1],
+                            along(p, k, 0),
+                        )
+                    )
+                flying[g]["first"].append(group)
+            return
         flying[g]["first"] = [
             [
                 copy(
@@ -440,8 +497,11 @@
     def go_second(g):
         flying[g]["second"] = []
         for p in range(3):
-            total = grads_ref[share_rows(g, core, p, here[p]), :].astype(F32)
-            for i in range(len(seven)):
+            if g < 2:
+                total = staged[g][1][p, rows(here[p] * SHARES[g], SHARES[g]), :].astype(F32)
+            else:
+                total = grads_ref[share_rows(g, core, p, here[p]), :].astype(F32)
+            for i in range(len(flying[g]["first"][p])):
                 flying[g]["first"][p][i].wait_recv()
                 total = total + steps[g][0][p, i].astype(F32)
             flying[g]["second"].append(spread_out(g, p, 1, low(total), (p + 1) % 3))
@@ -453,24 +513,46 @@
             flying[g]["third"].append(spread_out(g, p, 2, total, (p + 2) % 3))
 
     def go_back(g):
-        flying[g]["end"] = []
+        flying[g]["back"] = []
+        partners = [(k, 0) for k in range(1, SIDE)] if g < 2 else seven
         for p in range(3):
             at = share_rows(g, core, p, here[p])
             sum_ref[at, :] = gathered(flying[g]["third"][p], steps[g][2], p)
-            flying[g]["end"] += [
-                copy(
-                    sum_ref.at[at],
-                    sum_ref.at[at],
-                    send.at[g, 3, p, i],
-                    recv.at[g, 3, p, i],
-                    along(p, k, o),
+            flying[g]["back"].append(
+                [
+                    copy(
+                        sum_ref.at[at],
+                        sum_ref.at[at],
+                        send.at[g, 3, p, i],
+                        recv.at[g, 3, p, i],
+                        along(p, k, o),
+                    )
+                    for i, (k, o) in enumerate(partners)
+                ]
+            )
+
+    def go_end(g):
+        flying[g]["end"] = []
+        for p in range(3):
+            for c in flying[g]["back"][p]:
+                c.wait_recv()
+            if g < 2:
+                at = part_rows(g, core, p)
+                flying[g]["end"].append(
+                    copy(
+                        sum_ref.at[at],
+                        sum_ref.at[at],
+                        core_send.at[g, 3 + p],
+                        core_recv.at[g, 3 + p],
+                        sibling,
+                    )
                 )
-                for i, (k, o) in enumerate(seven)
-            ]
-
-    go_first(0)
-
-    def conv_back(b, carry):
+
+    go_core(0)
+
+    line = iota((1, TOK), 1) >> 4
+
+    def conv_back(b):
         total = None
         for dy in range(3):
             part = None
@@ -478,13 +560,13 @@
                 product = nt(wconv_ref[3 * dy + dx], tap(b, dy, dx))
                 part = product if part is None else part + product
             if dy != 1:
-                part = jnp.where((drop0, drop2)[dy // 2], 0.0, part)
+                part = jnp.where((line == (27, 28)[dy // 2]) & last_row, 0.0, part)
             total = part if total is None else total + part
-        dshift[b, :C, :] = low(total)
-        return carry
+        for i, u in enumerate(halves(b)):
+            dshift[u, :C, :] = low(total[:, i * UT : (i + 1) * UT])
 
     def back_to_heads(step, carry):
-        bs = (2 * step, 2 * step + 1)
+        bs = [4 * step + i for i in range(4)]
         d_pres = [low(nn(w2p[...], dshift[b]) * s_slope[b]) for b in bs]
         d_middles = []
         for b, d_pre in zip(bs, d_pres):
@@ -499,56 +581,66 @@
             dheads[b] = low(nn(wprojp[...], d_attn))
         return carry
 
-    lax.fori_loop(0, NBLK, conv_back, 0)
-    lax.fori_loop(0, NBLK // 2, back_to_heads, 0)
+    conv_back(0)
+    conv_back(1)
+    go_first(0)
+    conv_back(2)
+    conv_back(3)
+    lax.fori_loop(0, 2, back_to_heads, 0)
     go_second(0)
 
-    fc2 = over_blocks(lambda b: nt(dshift[b], s_hidden[b]))
-    fc1 = over_blocks(lambda b: nt(s_n2[b], s_dpre[b]))
+    fc2 = over_blocks(lambda b: nt(both(dshift, b), both(s_hidden, b)))
+    fc1 = over_blocks(lambda b: nt(both(s_n2, b), both(s_dpre, b)))
     for place, total in ((14, fc2), (17, fc1)):
         put_tile(place, total[:, :128])
         put_tile(place + 1, total[:, 128:256])
         put_pair(place + 2, total[:, 256:], jnp.zeros((CP, 384 - FF), F32))
-    proj = over_blocks(lambda b: nt(attended[b], s_dattn[b]))
+    proj = over_blocks(lambda b: nt(both(attended, b), both(s_dattn, b)))
     put_tile(20, proj[:, :128])
     put_pair(21, proj[:, 128:192], jnp.zeros((CP, 64), F32))
-    go_first(1)
-
-    def heads_back(b):
-        units = [(a, j) for a in range(ROWS // WIN) for j in range(HEADS // 2)]
-
-        def part(ref, third, a, j):
+    go_core(1)
+
+    def heads_back(step):
+        units = [
+            (u, a, j)
+            for u in (2 * step, 2 * step + 1)
+            for a in range(PAIRS)
+            for j in range(HEADS // 2)
+        ]
+
+        def part(ref, u, third, a, j):
             top = third * CP + 64 * j
-            return ref[b, top : top + 64, a * PAIR : (a + 1) * PAIR]
-
-        d_probs = {}
-        for a, j in units:
-            d_probs[a, j] = tn(part(packed, 2, a, j), two_heads(part(dheads, 0, a, j)))
-        p_all, s_all = {}, {}
-        for a, j in units:
+            return ref[u, top : top + 64, a * PAIR : (a + 1) * PAIR]
+
+        d_probs = [
+            tn(part(packed, u, 2, a, j), two_heads(part(dheads, u, 0, a, j))) for u, a, j in units
+        ]
+        wide = []
+        for (u, a, j), d_prob in zip(units, d_probs):
             p_wide, s_wide = [], []
             for s in range(2):
-                p = probs[b, a, 2 * j + s]
-                dp = fold(d_probs[a, j][:, s * PAIR : (s + 1) * PAIR], second)
+                p = probs[u, a, 2 * j + s]
+                dp = fold(d_prob[:, s * PAIR : (s + 1) * PAIR], second)
                 ds = p * (dp - jnp.sum(p * dp, axis=0, keepdims=True)) * factor
                 p_wide.append(unfold(p, second))
                 s_wide.append(unfold(ds, second))
-            p_all[a, j], s_all[a, j] = p_wide, s_wide
-        for a, j in units:
+            wide.append((p_wide, s_wide))
+        for (u, a, j), (p_wide, s_wide) in zip(units, wide):
             lanes = slice(a * PAIR, (a + 1) * PAIR)
-            dv = nt(part(dheads, 0, a, j), jnp.concatenate(p_all[a, j], axis=0))
-            dq = nn(part(packed, 1, a, j), jnp.concatenate(s_all[a, j], axis=1))
-            dk = nt(part(packed, 0, a, j), jnp.concatenate(s_all[a, j], axis=0))
-            dpacked[b, 64 * j : 64 * j + 64, lanes] = low(own_heads(dq))
-            dpacked[b, CP + 64 * j : CP + 64 * j + 64, lanes] = low(own_heads(dk))
-            dpacked[b, 2 * CP + 64 * j : 2 * CP + 64 * j + 64, lanes] = low(own_heads(dv))
+            dv = nt(part(dheads, u, 0, a, j), jnp.concatenate(p_wide, axis=0))
+            dq = nn(part(packed, u, 1, a, j), jnp.concatenate(s_wide, axis=1))
+            dk = nt(part(packed, u, 0, a, j), jnp.concatenate(s_wide, axis=0))
+            dpacked[u, 64 * j : 64 * j + 64, lanes] = low(own_heads(dq))
+            dpacked[u, CP + 64 * j : CP + 64 * j + 64, lanes] = low(own_heads(dk))
+            dpacked[u, 2 * CP + 64 * j : 2 * CP + 64 * j + 64, lanes] = low(own_heads(dv))
 
     heads_back(0)
+    go_first(1)
     heads_back(1)
+    heads_back(2)
     go_third(0)
-    heads_back(2)
     heads_back(3)
-    qkv = over_blocks(lambda b: nt(s_n1[b], dpacked[b]))
+    qkv = over_blocks(lambda b: nt(both(s_n1, b), both(dpacked, b)))
     for i in range(4):
         put_tile(22 + i, qkv[:, i * 128 : (i + 1) * 128])
     put_pair(26, qkv[:, 512:576], jnp.zeros((CP, 64), F32))
@@ -558,23 +650,28 @@
 
     ones_pair = eye(PAIR, PAIR)
 
-    def inputs_back(b):
-        d_in = s_dmid[b] + norm_back(nn(wqkvp[...], dpacked[b]), s_norm1[b], s_inv1[b], gain1)
-        d_low = low(d_in)
-        for a in range(ROWS // WIN):
-            natural = nt(ones_pair, d_low[:, a * PAIR : (a + 1) * PAIR])
-            d_ref[b, a * PAIR : (a + 1) * PAIR, :] = low(natural[:, :C])
-
-    inputs_back(NBLK - 1)
+    def inputs_back(*us):
+        d_ins = [
+            s_dmid[u] + norm_back(nn(wqkvp[...], dpacked[u]), s_norm1[u], s_inv1[u], gain1)
+            for u in us
+        ]
+        for u, d_in in zip(us, d_ins):
+            b, half = place_of(u)
+            d_low = low(d_in)
+            for a in range(PAIRS):
+                natural = nt(ones_pair, d_low[:, a * PAIR : (a + 1) * PAIR])
+                at = half * UT + a * PAIR
+                d_ref[b, at : at + PAIR, :] = low(natural[:, :C])
+
+    inputs_back(6, 7)
     edge = d_ref[NBLK - 1].astype(F32).reshape(ROWS, 2, 8, C)[:, 1]
     strip_out[...] = low(edge.reshape(ROWS * 8, C))
     leaving = [
         copy(strip_out.at[224:256], hc_ref, out_send.at[2], out_recv.at[2], (down, right)),
         copy(strip_out, hs_ref, out_send.at[1], out_recv.at[1], (row, right)),
     ]
-    inputs_back(0)
-    inputs_back(1)
-    inputs_back(2)
+    inputs_back(3, 4, 5)
+    inputs_back(0, 1, 2)
     leaving.append(
         copy(d_ref.at[:, 448:512, :], hr_ref, out_send.at[0], out_recv.at[0], (down, col))
     )
@@ -591,11 +688,14 @@
     go_back(0)
     go_second(2)
     go_third(1)
+    go_end(0)
     go_third(2)
     go_back(1)
     keep(0)
     go_back(2)
+    go_end(1)
     keep(1)
+    go_end(2)
     keep(2)
     for c in leaving:
         c.wait_recv()
@@ -606,8 +706,7 @@
 
 
 def call_layer(features, cotangent, w_qkv, w_proj, w_fc1, w_fc2_t, w_conv, g1, g2, table):
-    blocks = ROWS // WIN
-    reductions = []
+    reductions = [VMEM((3, n, 128), BF) for n in PARTS[:2] * 2]
     for slots in (2 * SIDE - 1, SIDE, SIDE):
         reductions += [VMEM((3, slots, n, 128), BF) for n in SHARES]
     inputs = (features, cotangent, w_qkv, w_proj, w_fc1, w_fc2_t, w_conv, g1, g2, table)
@@ -637,30 +736,32 @@
         VMEM((CP, FF), BF),
         VMEM((FF, CP), BF),
         VMEM((HEADS, WIN * WIN, PAIR), F32),
-        VMEM((NBLK, CP, TOK), F32),
-        VMEM((NBLK, 1, TOK), F32),
-        VMEM((NBLK, CP, TOK), BF),
-        VMEM((NBLK, 3 * CP, TOK), BF),
-        VMEM((NBLK, CP, TOK), BF),
-        VMEM((NBLK, blocks, HEADS, WIN * WIN, PAIR), F32),
-        VMEM((NBLK, CP, TOK), F32),
-        VMEM((NBLK, 1, TOK), F32),
-        VMEM((NBLK, CP, TOK), BF),
-        VMEM((NBLK, FF, TOK), F32),
-        VMEM((NBLK, FF, TOK), BF),
-        VMEM((3, NBLK, CP, TOK), BF),
-        VMEM((NBLK, CP, TOK), BF),
-        VMEM((NBLK, FF, TOK), BF),
-        VMEM((NBLK, CP, TOK), BF),
-        VMEM((NBLK, CP, TOK), BF),
-        VMEM((NBLK, 3 * CP, TOK), BF),
-        VMEM((NBLK, CP, TOK), F32),
+        VMEM((UNITS, CP, UT), F32),
+        VMEM((UNITS, 1, UT), F32),
+        VMEM((UNITS, CP, UT), BF),
+        VMEM((UNITS, 3 * CP, UT), BF),
+        VMEM((UNITS, CP, UT), BF),
+        VMEM((UNITS, PAIRS, HEADS, WIN * WIN, PAIR), F32),
+        VMEM((UNITS, CP, UT), F32),
+        VMEM((UNITS, 1, UT), F32),
+        VMEM((UNITS, CP, UT), BF),
+        VMEM((UNITS, FF, UT), F32),
+        VMEM((UNITS, FF, UT), BF),
+        VMEM((3, UNITS, CP, UT), BF),
+        VMEM((UNITS, CP, UT), BF),
+        VMEM((UNITS, FF, UT), BF),
+        VMEM((UNITS, CP, UT), BF),
+        VMEM((UNITS, CP, UT), BF),
+        VMEM((UNITS, 3 * CP, UT), BF),
+        VMEM((UNITS, CP, UT), F32),
         pltpu.SemaphoreType.DMA((10,)),
         pltpu.SemaphoreType.DMA((4,)),
         pltpu.SemaphoreType.DMA((6,)),
         pltpu.SemaphoreType.DMA((6,)),
         pltpu.SemaphoreType.DMA((3,)),
         pltpu.SemaphoreType.DMA((3,)),
+        pltpu.SemaphoreType.DMA((2, 6)),
+        pltpu.SemaphoreType.DMA((2, 6)),
         pltpu.SemaphoreType.DMA((3, 4, 3, 2 * SIDE - 1)),
         pltpu.SemaphoreType.DMA((3, 4, 3, 2 * SIDE - 1)),
     ]

time: 66.6 us -> 63.4 us (0.952)
  Pallas kernels: 65.6 us -> 62.4 us
    pallas_call x1, Pallas kernels: 61.6 us -> 58.4 us  [call_layer(): pl.pallas_call(layer, out_shape=(jax.ShapeDtypeStruct((NBLK, TOK, C), BF)...]
where the time goes in v4:
time: 63.4 us; the launch traced here: 63.2 us
  Pallas kernels  62.4 us (98%)
  between operations  0.8 us (1%)
    pallas_call x1, Pallas kernels, call_layer(): pl.pallas_call(layer, out_shape=(jax.ShapeDtypeStruct((NBLK, TOK, C), BF)...  58.4 us
    pallas_call x1, Pallas kernels, call_results(): pl.pallas_call(results, out_shape=shapes, in_specs=[pl.BlockSpec(memory_s...  4 us

profile of v4, /device:TPU:1, one launch (start us, length us, event | category | flops | bytes accessed | tf_op | source)
XLA Modules:
  0.0 63.2 jit_solution(627937597029711099)
XLA Ops:
  0.6 58.4 %layer.1 = (bf16[4,512,180]{2,1,0:T(8,128)(2,1)}, bf16[5376,128]{1,0:T(8,128)(2,1)}, bf16[4,64,180]{2,1,0:T(8,128)(2,1)}, bf16[256,180]{1,0:T(8,128)(2,1)}, bf16[32,180]{1,0:T(8,128)(2,1)}) custom-call(bf16[32,64,180]{2,1,0:T(8,128)(2,1)} %f_hbm.1, bf16[32,64,180]{2,1,0:T(8,128)(2,1)} %g_hbm.1, bf16[180,540]{1,0:T(8,128)(2,1)} %wqkv_hbm.1, ...), custom_call_target="tpu_custom_call" | custom-call | tf_op jit(solution)/shard_map/layer/pallas_call | solution.py:768
  59.1 4.0 %results.1 = (bf16[32,64,180]{2,1,0:T(8,128)(2,1)}, f32[180,540]{1,0:T(8,128)}, f32[180,180]{1,0:T(8,128)}, f32[180,360]{1,0:T(8,128)}, f32[180,360]{1,0:T(8,128)}, /*index=5*/f32[9,180,180]{2,1,0:T(8,128)}) custom-call(bf16[4,512,180]{2,1,0:T(8,128)(2,1)} %get-tuple-element.17.d_hbm, bf16[4,64,180]{2,1,0:T(8,128)(2,1)} %get-tuple-element.18.hr_hbm, ...), custom_call_target="tpu_custom_call" | custom-call | tf_op jit(solution)/shard_map/results/pallas_call | solution.py:861

commit v5 on v4

--- a/solution.py
+++ b/solution.py
@@ -581,13 +581,10 @@
             dheads[b] = low(nn(wprojp[...], d_attn))
         return carry
 
-    conv_back(0)
-    conv_back(1)
+    for b in range(NBLK):
+        conv_back(b)
     go_first(0)
-    conv_back(2)
-    conv_back(3)
     lax.fori_loop(0, 2, back_to_heads, 0)
-    go_second(0)
 
     fc2 = over_blocks(lambda b: nt(both(dshift, b), both(s_hidden, b)))
     fc1 = over_blocks(lambda b: nt(both(s_n2, b), both(s_dpre, b)))
@@ -635,10 +632,10 @@
             dpacked[u, 2 * CP + 64 * j : 2 * CP + 64 * j + 64, lanes] = low(own_heads(dv))
 
     heads_back(0)
+    go_second(0)
+    heads_back(1)
     go_first(1)
-    heads_back(1)
     heads_back(2)
-    go_third(0)
     heads_back(3)
     qkv = over_blocks(lambda b: nt(both(s_n1, b), both(dpacked, b)))
     for i in range(4):
@@ -646,7 +643,7 @@
     put_pair(26, qkv[:, 512:576], jnp.zeros((CP, 64), F32))
     put_tile(27, jnp.zeros((CP, 128), F32))
     go_first(2)
-    go_second(1)
+    go_third(0)
 
     ones_pair = eye(PAIR, PAIR)
 
@@ -664,12 +661,16 @@
                 d_ref[b, at : at + PAIR, :] = low(natural[:, :C])
 
     inputs_back(6, 7)
-    edge = d_ref[NBLK - 1].astype(F32).reshape(ROWS, 2, 8, C)[:, 1]
-    strip_out[...] = low(edge.reshape(ROWS * 8, C))
+    edge = d_ref[NBLK - 1].astype(F32).reshape(ROWS // 2, 2, 2, 8, C)[:, :, 1]
+    pairs = jnp.where(
+        iota((ROWS // 2, 8, C), 1) < 4, pltpu.roll(edge[:, 0], 4, 1), edge[:, 1]
+    )
+    strip_out[...] = low(pairs.reshape(ROWS * 4, C))
     leaving = [
-        copy(strip_out.at[224:256], hc_ref, out_send.at[2], out_recv.at[2], (down, right)),
+        copy(strip_out.at[112:128], hc_ref, out_send.at[2], out_recv.at[2], (down, right)),
         copy(strip_out, hs_ref, out_send.at[1], out_recv.at[1], (row, right)),
     ]
+    go_second(1)
     inputs_back(3, 4, 5)
     inputs_back(0, 1, 2)
     leaving.append(
@@ -685,17 +686,17 @@
         stores.append(pltpu.make_async_copy(sum_ref.at[at], sum_hbm.at[at], store.at[1 + g]))
         stores[-1].start()
 
+    go_second(2)
     go_back(0)
-    go_second(2)
     go_third(1)
+    go_third(2)
     go_end(0)
-    go_third(2)
     go_back(1)
+    go_back(2)
     keep(0)
-    go_back(2)
     go_end(1)
+    go_end(2)
     keep(1)
-    go_end(2)
     keep(2)
     for c in leaving:
         c.wait_recv()
@@ -722,7 +723,7 @@
         VMEM((48, C), BF),
         VMEM((ROWS * 4, C), BF),
         VMEM((ROWS * 8, C), BF),
-        VMEM((256, C), BF),
+        VMEM((ROWS * 4, C), BF),
         VMEM((GROWS, 128), BF),
         *reductions,
         VMEM((NBLK, TOK, C), BF),
@@ -771,8 +772,8 @@
             jax.ShapeDtypeStruct((NBLK, TOK, C), BF),
             jax.ShapeDtypeStruct((GROWS, 128), BF),
             jax.ShapeDtypeStruct((NBLK, 64, C), BF),
-            jax.ShapeDtypeStruct((256, C), BF),
-            jax.ShapeDtypeStruct((32, C), BF),
+            jax.ShapeDtypeStruct((ROWS * 4, C), BF),
+            jax.ShapeDtypeStruct((16, C), BF),
         ),
         in_specs=[pl.BlockSpec(memory_space=pl.ANY)] * 10,
         out_specs=[pl.BlockSpec(memory_space=pl.ANY)] * 2 + [pl.BlockSpec(memory_space=VMEM)] * 3,
@@ -804,17 +805,17 @@
     for c in loads[:4]:
         c.wait()
     sub = iota((8, C), 0)
-    extras = hs_ref[...].astype(F32).reshape(ROWS, 8, C)
-    corners = hc_ref[...].astype(F32).reshape(4, 8, C)
+    extras = hs_ref[...].astype(F32).reshape(ROWS // 2, 8, C)
+    corners = hc_ref[...].astype(F32).reshape(2, 8, C)
     for i in range(ROWS):
         if i < 4:
             pieces = [hr_ref[b, i * BLK : (i + 1) * BLK, :] for b in range(NBLK)]
-            extra = corners[i]
+            extra = corners[i // 2]
         else:
             pieces = [d_ref[b, (i - 4) * BLK : (i - 3) * BLK, :] for b in range(NBLK)]
-            extra = extras[i - 4]
+            extra = extras[(i - 4) // 2]
         v = pltpu.roll(jnp.concatenate(pieces, axis=0).astype(F32), 4, 0)
-        head = jnp.where(sub < 4, pltpu.roll(extra, 4, 0), v[:8])
+        head = jnp.where(sub < 4, pltpu.roll(extra, 4, 0) if i % 2 else extra, v[:8])
         out_ref[i] = low(jnp.concatenate([head, v[8:]], axis=0))
 
     keep(out_ref, out_hbm)

time: 63.4 us -> 63 us (level)
  no operation moved by 1% of the time
where the time goes in v5:
time: 63 us; the launch traced here: 62.8 us
  Pallas kernels  62 us (98%)
  between operations  0.8 us (1%)
    pallas_call x1, Pallas kernels, call_layer(): pl.pallas_call(layer, out_shape=(jax.ShapeDtypeStruct((NBLK, TOK, C), BF)...  58.1 us
    pallas_call x1, Pallas kernels, call_results(): pl.pallas_call(results, out_shape=shapes, in_specs=[pl.BlockSpec(memory_s...  3.97 us

profile of v5, /device:TPU:1, one launch (start us, length us, event | category | flops | bytes accessed | tf_op | source)
XLA Modules:
  0.0 62.8 jit_solution(15083529328712895925)
XLA Ops:
  0.6 58.1 %layer.1 = (bf16[4,512,180]{2,1,0:T(8,128)(2,1)}, bf16[5376,128]{1,0:T(8,128)(2,1)}, bf16[4,64,180]{2,1,0:T(8,128)(2,1)}, bf16[128,180]{1,0:T(8,128)(2,1)}, bf16[16,180]{1,0:T(8,128)(2,1)}) custom-call(bf16[32,64,180]{2,1,0:T(8,128)(2,1)} %f_hbm.1, bf16[32,64,180]{2,1,0:T(8,128)(2,1)} %g_hbm.1, bf16[180,540]{1,0:T(8,128)(2,1)} %wqkv_hbm.1, ...), custom_call_target="tpu_custom_call" | custom-call | tf_op jit(solution)/shard_map/layer/pallas_call | solution.py:769
  58.7 4.0 %results.1 = (bf16[32,64,180]{2,1,0:T(8,128)(2,1)}, f32[180,540]{1,0:T(8,128)}, f32[180,180]{1,0:T(8,128)}, f32[180,360]{1,0:T(8,128)}, f32[180,360]{1,0:T(8,128)}, /*index=5*/f32[9,180,180]{2,1,0:T(8,128)}) custom-call(bf16[4,512,180]{2,1,0:T(8,128)(2,1)} %get-tuple-element.17.d_hbm, bf16[4,64,180]{2,1,0:T(8,128)(2,1)} %get-tuple-element.18.hr_hbm, ...), custom_call_target="tpu_custom_call" | custom-call | tf_op jit(solution)/shard_map/results/pallas_call | solution.py:862

commit v6 on v5

--- a/solution.py
+++ b/solution.py
@@ -132,7 +132,7 @@
     fr_ref, gr_ref, fstrip_ref, gstrip_ref, fcorner_ref, gcorner_ref,
     fstrip_in, gstrip_in, strip_out,
     grads_ref, core0, core1, held0, held1, first0, first1, first2, second0, second1, second2, third0, third1, third2,
-    xs, gs, wqkvt, wqkvp, wprojt, wprojp, w1t, w1p, w2t, w2p, bias,
+    xs, gs, wqkvt, wqkvp, wprojt, wprojp, w1t, w1p, w2t, w2p, offsets, bias,
     s_norm1, s_inv1, s_n1, packed, attended, probs, s_norm2, s_inv2, s_n2, s_slope, s_hidden, s_z,
     dshift, s_dpre, s_dattn, dheads, dpacked, s_dmid,
     load, store, in_send, in_recv, out_send, out_recv, core_send, core_recv, send, recv,
@@ -261,10 +261,12 @@
         pick = low(jnp.where(hit, 1.0, 0.0))
         line = nn(high, pick) + nn(mid, pick) + nn(rest_piece, pick)
         for h in range(HEADS):
-            for kr in range(WIN):
-                start = (WIN - 1 - kr) * BLK
-                at = kr * WIN + kc
-                bias[h, at : at + 1, :] = line[h : h + 1, start : start + PAIR]
+            offsets[h, kc : kc + 1, :] = line[h : h + 1]
+    for h in range(HEADS):
+        by_key = offsets[h]
+        for kr in range(WIN):
+            start = (WIN - 1 - kr) * BLK
+            bias[h, kr * WIN : (kr + 1) * WIN, :] = by_key[:, start : start + PAIR]
     dshift[...] = jnp.zeros_like(dshift)
 
     def last_rows():
@@ -565,8 +567,8 @@
         for i, u in enumerate(halves(b)):
             dshift[u, :C, :] = low(total[:, i * UT : (i + 1) * UT])
 
-    def back_to_heads(step, carry):
-        bs = [4 * step + i for i in range(4)]
+    def back_to_heads():
+        bs = range(UNITS)
         d_pres = [low(nn(w2p[...], dshift[b]) * s_slope[b]) for b in bs]
         d_middles = []
         for b, d_pre in zip(bs, d_pres):
@@ -579,12 +581,13 @@
         for b, d_attn in zip(bs, d_middles):
             s_dattn[b] = d_attn
             dheads[b] = low(nn(wprojp[...], d_attn))
-        return carry
-
-    for b in range(NBLK):
-        conv_back(b)
+
+    conv_back(0)
+    conv_back(1)
     go_first(0)
-    lax.fori_loop(0, 2, back_to_heads, 0)
+    conv_back(2)
+    conv_back(3)
+    back_to_heads()
 
     fc2 = over_blocks(lambda b: nt(both(dshift, b), both(s_hidden, b)))
     fc1 = over_blocks(lambda b: nt(both(s_n2, b), both(s_dpre, b)))
@@ -596,6 +599,7 @@
     put_tile(20, proj[:, :128])
     put_pair(21, proj[:, 128:192], jnp.zeros((CP, 64), F32))
     go_core(1)
+    go_second(0)
 
     def heads_back(step):
         units = [
@@ -632,18 +636,17 @@
             dpacked[u, 2 * CP + 64 * j : 2 * CP + 64 * j + 64, lanes] = low(own_heads(dv))
 
     heads_back(0)
-    go_second(0)
     heads_back(1)
     go_first(1)
     heads_back(2)
     heads_back(3)
+    go_third(0)
     qkv = over_blocks(lambda b: nt(both(s_n1, b), both(dpacked, b)))
     for i in range(4):
         put_tile(22 + i, qkv[:, i * 128 : (i + 1) * 128])
     put_pair(26, qkv[:, 512:576], jnp.zeros((CP, 64), F32))
     put_tile(27, jnp.zeros((CP, 128), F32))
     go_first(2)
-    go_third(0)
 
     ones_pair = eye(PAIR, PAIR)
 
@@ -686,8 +689,8 @@
         stores.append(pltpu.make_async_copy(sum_ref.at[at], sum_hbm.at[at], store.at[1 + g]))
         stores[-1].start()
 
+    go_back(0)
     go_second(2)
-    go_back(0)
     go_third(1)
     go_third(2)
     go_end(0)
@@ -736,6 +739,7 @@
         VMEM((CP, FF), BF),
         VMEM((CP, FF), BF),
         VMEM((FF, CP), BF),
+        VMEM((HEADS, WIN, 15 * BLK), F32),
         VMEM((HEADS, WIN * WIN, PAIR), F32),
         VMEM((UNITS, CP, UT), F32),
         VMEM((UNITS, 1, UT), F32),
@@ -789,12 +793,12 @@
     d_hbm, hr_hbm, hs_hbm, hc_hbm, sum_hbm,
     out_hbm, qkv_hbm, proj_hbm, fc1_hbm, fc2_hbm, conv_hbm,
     d_ref, hr_ref, hs_ref, hc_ref, sum_ref,
-    out_ref, qkv_ref, proj_ref, fc1_ref, fc2_ref, conv_ref, load, store,
+    out_ref, qkv_ref, proj_ref, fc1_ref, fc2_ref, conv_ref, sel_ref, load, store,
 ):
     hbm = (hr_hbm, hs_hbm, hc_hbm, d_hbm, sum_hbm)
     own = (hr_ref, hs_ref, hc_ref, d_ref, sum_ref)
     loads = [pltpu.make_async_copy(s, t, load.at[i]) for i, (s, t) in enumerate(zip(hbm, own))]
-    for c in loads:
+    for c in (loads[4], *loads[:4]):
         c.start()
     stores = []
 
@@ -802,6 +806,22 @@
         stores.append(pltpu.make_async_copy(source, target, store.at[len(stores)]))
         stores[-1].start()
 
+    sel_ref[...] = spread(3 * CP, 3 * C, 0)
+    loads[4].wait()
+    scale = 1.0 / math.sqrt(ROWS * COLS * lax.axis_size("row") * lax.axis_size("col"))
+
+    def full(i):
+        return sum_ref[i * CP : (i + 1) * CP, :]
+
+    def rest(i):
+        return full(9 + i // 2)[:, 64 * (i % 2) : 64 * (i % 2) + 64]
+
+    def square(i, r):
+        return jnp.concatenate([full(i), rest(r)], axis=1)
+
+    for t in range(9):
+        conv_ref[t] = square(t, t).astype(F32)[:C, :C] * scale
+    keep(conv_ref, conv_hbm)
     for c in loads[:4]:
         c.wait()
     sub = iota((8, C), 0)
@@ -819,21 +839,6 @@
         out_ref[i] = low(jnp.concatenate([head, v[8:]], axis=0))
 
     keep(out_ref, out_hbm)
-    loads[4].wait()
-    scale = 1.0 / math.sqrt(ROWS * COLS * lax.axis_size("row") * lax.axis_size("col"))
-
-    def full(i):
-        return sum_ref[i * CP : (i + 1) * CP, :]
-
-    def rest(i):
-        return full(9 + i // 2)[:, 64 * (i % 2) : 64 * (i % 2) + 64]
-
-    def square(i, r):
-        return jnp.concatenate([full(i), rest(r)], axis=1)
-
-    for t in range(9):
-        conv_ref[t] = square(t, t).astype(F32)[:C, :C] * scale
-    keep(conv_ref, conv_hbm)
     proj_ref[...] = nn(spread(CP, C, 1), jnp.concatenate([full(20), full(21)[:, :64]], axis=1))[:, :C] * scale
     keep(proj_ref, proj_hbm)
     fc2 = jnp.concatenate([full(14), full(15), full(16)], axis=1).astype(F32)
@@ -843,7 +848,7 @@
     fc1_ref[...] = fc1[:C, :FF] * scale
     keep(fc1_ref, fc1_hbm)
     qkv = jnp.concatenate([full(22), full(23), full(24), full(25), full(26)[:, :64]], axis=1)
-    qkv_ref[...] = nn(qkv, spread(3 * CP, 3 * C, 0))[:C] * scale
+    qkv_ref[...] = nn(qkv, sel_ref[...])[:C] * scale
     keep(qkv_ref, qkv_hbm)
     for c in stores:
         c.wait()
@@ -866,6 +871,7 @@
         out_specs=[pl.BlockSpec(memory_space=pl.ANY)] * 6,
         scratch_shapes=[
             *(VMEM(v.shape, v.dtype) for v in operands + shapes),
+            VMEM((3 * CP, 3 * C), BF),
             pltpu.SemaphoreType.DMA((5,)),
             pltpu.SemaphoreType.DMA((6,)),
         ],

time: 63 us -> 61 us (0.968)
  Pallas kernels: 62 us -> 60 us
    pallas_call x1, Pallas kernels: 58.1 us -> 56.2 us  [call_layer(): pl.pallas_call(layer, out_shape=(jax.ShapeDtypeStruct((NBLK, TOK, C), BF)...]
where the time goes in v6:
time: 61 us; the launch traced here: 60.8 us
  Pallas kernels  60 us (98%)
  between operations  0.8 us (1%)
    pallas_call x1, Pallas kernels, call_layer(): pl.pallas_call(layer, out_shape=(jax.ShapeDtypeStruct((NBLK, TOK, C), BF)...  56.2 us
    pallas_call x1, Pallas kernels, call_results(): pl.pallas_call(results, out_shape=shapes, in_specs=[pl.BlockSpec(memory_s...  3.79 us

profile of v6, /device:TPU:1, one launch (start us, length us, event | category | flops | bytes accessed | tf_op | source)
XLA Modules:
  0.0 60.8 jit_solution(6107695027318750582)
XLA Ops:
  0.6 56.2 %layer.1 = (bf16[4,512,180]{2,1,0:T(8,128)(2,1)}, bf16[5376,128]{1,0:T(8,128)(2,1)}, bf16[4,64,180]{2,1,0:T(8,128)(2,1)}, bf16[128,180]{1,0:T(8,128)(2,1)}, bf16[16,180]{1,0:T(8,128)(2,1)}) custom-call(bf16[32,64,180]{2,1,0:T(8,128)(2,1)} %f_hbm.1, bf16[32,64,180]{2,1,0:T(8,128)(2,1)} %g_hbm.1, bf16[180,540]{1,0:T(8,128)(2,1)} %wqkv_hbm.1, ...), custom_call_target="tpu_custom_call" | custom-call | tf_op jit(solution)/shard_map/layer/pallas_call | solution.py:773
  56.9 3.8 %results.1 = (bf16[32,64,180]{2,1,0:T(8,128)(2,1)}, f32[180,540]{1,0:T(8,128)}, f32[180,180]{1,0:T(8,128)}, f32[180,360]{1,0:T(8,128)}, f32[180,360]{1,0:T(8,128)}, /*index=5*/f32[9,180,180]{2,1,0:T(8,128)}) custom-call(bf16[4,512,180]{2,1,0:T(8,128)(2,1)} %get-tuple-element.17.d_hbm, bf16[4,64,180]{2,1,0:T(8,128)(2,1)} %get-tuple-element.18.hr_hbm, ...), custom_call_target="tpu_custom_call" | custom-call | tf_op jit(solution)/shard_map/results/pallas_call | solution.py:867

commit v7 on v6

--- a/solution.py
+++ b/solution.py
@@ -327,13 +327,19 @@
         soft = []
         for (b, a, j), score in zip(units, scores):
             block, half = place_of(b)
-            row_flag = last_row & (half * PAIRS + a == ROWS // WIN - 1)
-            col_flag = last_col & (block == NBLK - 1)
-            mask = jnp.where((rows_differ & row_flag) | (cols_differ & col_flag), -100.0, 0.0)
+            differ = []
+            if half * PAIRS + a == ROWS // WIN - 1:
+                differ.append(rows_differ & last_row)
+            if block == NBLK - 1:
+                differ.append(cols_differ & last_col)
+            if differ:
+                mask = jnp.where(differ[0] | differ[-1], -100.0, 0.0)
             wide = []
             for s in range(2):
                 sc = fold(score[:, s * PAIR : (s + 1) * PAIR], second)
-                sc = sc * factor + bias[2 * j + s] + mask
+                sc = sc * factor + bias[2 * j + s]
+                if differ:
+                    sc = sc + mask
                 e = jnp.exp(sc - jnp.max(sc, axis=0, keepdims=True))
                 p = e * (1.0 / jnp.sum(e, axis=0, keepdims=True))
                 probs[b, a, 2 * j + s] = p
@@ -359,8 +365,9 @@
             drop0, drop2 = drops(half)
             z = middle + nn(w2t[...], s_hidden[b])
             s_z[1, b] = low(z)
-            s_z[0, b] = low(jnp.where(drop0, 0.0, z))
-            s_z[2, b] = low(jnp.where(drop2, 0.0, z))
+            if half == 1:
+                s_z[0, b] = low(jnp.where(drop0, 0.0, z))
+                s_z[2, b] = low(jnp.where(drop2, 0.0, z))
 
     forward(0, 1, 2)
     last_rows()
@@ -388,6 +395,11 @@
     def both(ref, b):
         return jnp.concatenate([ref[u] for u in halves(b)], axis=1)
 
+    def edged(dy, b):
+        return jnp.concatenate(
+            [s_z[dy if place_of(u)[1] == 1 else 1, u] for u in halves(b)], axis=1
+        )
+
     def over_blocks(term):
         total = term(0)
         for b in range(1, NBLK):
@@ -402,7 +414,7 @@
 
     held_back = None
     for t in range(9):
-        total = over_blocks(lambda b: nn(both(s_z.at[t // 3], b), tap(b, t // 3, t % 3)))
+        total = over_blocks(lambda b: nn(edged(t // 3, b), tap(b, t // 3, t % 3)))
         put_tile(t, total[:, :128])
         narrow = jnp.concatenate([total[:, 128:], jnp.zeros((CP, 256 - 12 - C), F32)], axis=1)
         narrow = narrow[:, :64]
@@ -604,7 +616,7 @@
     def heads_back(step):
         units = [
             (u, a, j)
-            for u in (2 * step, 2 * step + 1)
+            for u in range(4 * step, 4 * step + 4)
             for a in range(PAIRS)
             for j in range(HEADS // 2)
         ]
@@ -636,10 +648,8 @@
             dpacked[u, 2 * CP + 64 * j : 2 * CP + 64 * j + 64, lanes] = low(own_heads(dv))
 
     heads_back(0)
+    go_first(1)
     heads_back(1)
-    go_first(1)
-    heads_back(2)
-    heads_back(3)
     go_third(0)
     qkv = over_blocks(lambda b: nt(both(s_n1, b), both(dpacked, b)))
     for i in range(4):
@@ -674,8 +684,7 @@
         copy(strip_out, hs_ref, out_send.at[1], out_recv.at[1], (row, right)),
     ]
     go_second(1)
-    inputs_back(3, 4, 5)
-    inputs_back(0, 1, 2)
+    inputs_back(0, 1, 2, 3, 4, 5)
     leaving.append(
         copy(d_ref.at[:, 448:512, :], hr_ref, out_send.at[0], out_recv.at[0], (down, col))
     )

time: 61 us -> 60.9 us (level)
  no operation moved by 1% of the time
where the time goes in v7:
time: 60.9 us; the launch traced here: 60.8 us
  Pallas kernels  60 us (99%)
  between operations  0.8 us (1%)
    pallas_call x1, Pallas kernels, call_layer(): pl.pallas_call(layer, out_shape=(jax.ShapeDtypeStruct((NBLK, TOK, C), BF)...  56.2 us
    pallas_call x1, Pallas kernels, call_results(): pl.pallas_call(results, out_shape=shapes, in_specs=[pl.BlockSpec(memory_s...  3.79 us

profile of v7, /device:TPU:1, one launch (start us, length us, event | category | flops | bytes accessed | tf_op | source)
XLA Modules:
  0.0 60.8 jit_solution(2893626855102186659)
XLA Ops:
  0.6 56.2 %layer.1 = (bf16[4,512,180]{2,1,0:T(8,128)(2,1)}, bf16[5376,128]{1,0:T(8,128)(2,1)}, bf16[4,64,180]{2,1,0:T(8,128)(2,1)}, bf16[128,180]{1,0:T(8,128)(2,1)}, bf16[16,180]{1,0:T(8,128)(2,1)}) custom-call(bf16[32,64,180]{2,1,0:T(8,128)(2,1)} %f_hbm.1, bf16[32,64,180]{2,1,0:T(8,128)(2,1)} %g_hbm.1, bf16[180,540]{1,0:T(8,128)(2,1)} %wqkv_hbm.1, ...), custom_call_target="tpu_custom_call" | custom-call | tf_op jit(solution)/shard_map/layer/pallas_call | solution.py:782
  56.8 3.8 %results.1 = (bf16[32,64,180]{2,1,0:T(8,128)(2,1)}, f32[180,540]{1,0:T(8,128)}, f32[180,180]{1,0:T(8,128)}, f32[180,360]{1,0:T(8,128)}, f32[180,360]{1,0:T(8,128)}, /*index=5*/f32[9,180,180]{2,1,0:T(8,128)}) custom-call(bf16[4,512,180]{2,1,0:T(8,128)(2,1)} %get-tuple-element.17.d_hbm, bf16[4,64,180]{2,1,0:T(8,128)(2,1)} %get-tuple-element.18.hr_hbm, ...), custom_call_target="tpu_custom_call" | custom-call | tf_op jit(solution)/shard_map/results/pallas_call | solution.py:876
